TPU v7x, 32 devices: a whole 2x2x4 slice. The times are simulated.
32 devices in a mesh: var: 4 (over z), own: 4 (over y, x), sub: 2 (over core).
Axes of the slice: x: 2, y: 2, z: 4, core: 2. Of those that a mesh axis runs over, the one named last changes fastest.
Arguments:
- capacity_blocks: bfloat16 [2048, 5, 128, 128], P(('var', 'own', 'sub')), may hold values from -0.078125 to 0.078125
- capacity_rows: int32 [2048, 5], P(('var', 'own', 'sub')), may hold values from 0 to 7, all different within a row
- cover_self: bfloat16 [2048, 128, 128], P(('var', 'own', 'sub')), may hold values from -0.5 to 0.5
- cover_prev: bfloat16 [2048, 128, 128], P(('var', 'own', 'sub')), may hold values from -0.5 to 0.5
- scaling: bfloat16 [2048, 128], P(('var', 'own', 'sub')), may hold values from 0.099609375 to 10
Outputs:
- cover_diag: bfloat16 [2048, 128, 128], P(('var', 'own', 'sub'))
- cover_lower: bfloat16 [2048, 128, 128], P(('var', 'own', 'sub'))
- capacity_normal: float32 [1024, 1024], P(('var', 'own', 'sub'))
Inputs may be any that keep to these rules, and one draw needn't show every extreme that they name: `capacity_rows`: each column block names 5 different capacity row blocks, and every capacity row block is named somewhere.
All inputs are finite; a program needn't handle non-finite values.
Results may differ from a plain program's by a relative error of at most 0.0049.
Values may be sent and summed in bfloat16 or wider, within the bound.
No kernel may reach another device: no remote copies, remote signals or barrier semaphores. Data moves between devices by JAX's collectives and lax.ppermute only.
A program may use at most 192 MiB of HBM per device.

v0:
```python
import functools

import jax
import jax.numpy as jnp
from jax import lax
from jax.experimental import pallas as pl
from jax.experimental.pallas import tpu as pltpu
from jax.sharding import PartitionSpec as P

CAP = 8
AXES = ("var", "own", "sub")
NT = (((1,), (1,)), ((), ()))
F32, BF16 = jnp.float32, jnp.bfloat16


def swap(value, axis, mask):
    count = lax.axis_size(axis)
    return lax.ppermute(value, axis, [(i, i ^ mask) for i in range(count)])


def shifted(value, axis, steps):
    count = lax.axis_size(axis)
    return lax.ppermute(value, axis, [(i, i + steps) for i in range(count - steps)])


def send_order(axis):
    masks = list(range(1, lax.axis_size(axis)))
    return masks[1:] + masks[:1] if axis == "var" else masks[::-1]


def set_bits(mask, count):
    found = []
    for _ in range(count):
        low = mask & (-mask)
        found.append(31 - lax.clz(low))
        mask = mask ^ low
    return found


def capacity_kernel(step, parts, sizes, rows_ref, cap_ref, scale_ref, *rest):
    outs, (dense, scale_in, scale, acc, sems, scale_sem) = rest[: 2 * len(parts)], rest[2 * len(parts) :]
    count, width = cap_ref.shape[0], cap_ref.shape[2]
    nz = cap_ref.shape[1] // width
    turns = count // step
    side = acc.shape[0]
    tile = 2 * width

    def spot(r):
        return pl.ds(pl.multiple_of(r * width, width), width)

    def lay(k, carry):
        mask = jnp.int32(0)
        for p in range(nz):
            r = rows_ref[p, k]
            mask = mask | jnp.left_shift(jnp.int32(1), r)
            pltpu.make_async_copy(
                cap_ref.at[k, pl.ds(p * width, width), :], dense.at[k, spot(r), :], sems.at[k // step]
            ).start()
        for r in set_bits((1 << CAP) - 1 - mask, CAP - nz):
            dense[k, spot(r), :] = jnp.zeros((width, width), BF16)
        return carry

    fetch = pltpu.make_async_copy(scale_ref, scale_in, scale_sem)
    fetch.start()
    lax.fori_loop(0, count, lay, 0, unroll=4)
    fetch.wait()
    scale[...] = scale_in[...].astype(F32)
    acc[...] = jnp.zeros_like(acc)

    def turn(t, carry):
        first = t * step
        pltpu.make_async_copy(
            cap_ref.at[pl.ds(first, step)],
            dense.at[pl.ds(first, step), pl.ds(0, nz * width), :],
            sems.at[t],
        ).wait()
        ks = [first + i for i in range(step)]
        for j in range(side // tile):
            right = jnp.concatenate(
                [dense[k, pl.ds(tile * j, tile), :] * scale[pl.ds(k, 1), :].astype(BF16) for k in ks], axis=1
            )
            left = jnp.concatenate([dense[k, pl.ds(0, tile * (j + 1)), :] for k in ks], axis=1)
            acc[pl.ds(0, tile * (j + 1)), pl.ds(tile * j, tile)] += lax.dot_general(
                left, right, NT, preferred_element_type=F32
            )
        return carry

    lax.fori_loop(0, turns, turn, 0)
    for i in range(side // tile):
        for j in range(i):
            acc[pl.ds(tile * i, tile), pl.ds(tile * j, tile)] = acc[pl.ds(tile * j, tile), pl.ds(tile * i, tile)].T
    var, own, sub = (lax.axis_index(a) for a in AXES)
    n_var, n_own, held = sizes
    for at, (low, high, first) in enumerate(parts):
        keep_ref, send_ref = outs[2 * at], outs[2 * at + 1]
        for m in range(n_own):

            def emit(v, carry, m=m):
                chip = (var ^ v) * n_own + (own ^ m)
                mine = pl.ds(pl.multiple_of((2 * chip + sub) * held, held), held)
                other = pl.ds(pl.multiple_of((2 * chip + 1 - sub) * held, held), held)
                slot = (m, v) if first == "own" else (v, m)
                keep_ref[slot] = acc[mine, pl.ds(low, high - low)]
                send_ref[slot] = acc[other, pl.ds(low, high - low)].astype(send_ref.dtype)
                return carry

            lax.fori_loop(0, n_var, emit, 0, unroll=True)


def capacity(capacity_blocks, capacity_rows, scaling, parts):
    count, nz, width = capacity_blocks.shape[:3]
    n_var, n_own, n_sub = (lax.axis_size(a) for a in AXES)
    side = CAP * width
    held = side // (n_var * n_own * n_sub)
    step = 32
    sent = BF16 if held % 16 == 0 else F32
    shapes = []
    for low, high, first in parts:
        lead = (n_own, n_var) if first == "own" else (n_var, n_own)
        shapes += [jax.ShapeDtypeStruct(lead + (held, high - low), t) for t in (F32, sent)]
    hbm = pl.BlockSpec(memory_space=pltpu.HBM)
    smem, vmem = pl.BlockSpec(memory_space=pltpu.SMEM), pl.BlockSpec(memory_space=pltpu.VMEM)
    operands = (capacity_rows.T, capacity_blocks.reshape(count, nz * width, width), scaling)
    flops = 2 * side * side * count * width * 5 // 8
    outs = pl.pallas_call(
        functools.partial(capacity_kernel, step, parts, (n_var, n_own, held)),
        out_shape=shapes,
        in_specs=[smem, hbm, hbm],
        out_specs=[vmem] * len(shapes),
        scratch_shapes=[
            pltpu.VMEM((count, side, width), BF16),
            pltpu.VMEM((count, width), BF16),
            pltpu.VMEM((count, width), F32),
            pltpu.VMEM((side, side), F32),
            pltpu.SemaphoreType.DMA((count // step,)),
            pltpu.SemaphoreType.DMA,
        ],
        compiler_params=pltpu.CompilerParams(vmem_limit_bytes=32 * 2**20),
        cost_estimate=pl.CostEstimate(flops=flops, bytes_accessed=14 * 2**20, transcendentals=0),
        name="capacity",
    )(*(pltpu.with_memory_space_constraint(x, pltpu.HBM) for x in operands))
    return [(keep, send.astype(BF16)) for keep, send in zip(outs[0::2], outs[1::2])]


def cover_kernel(group, self_ref, prev_ref, scale_ref, diag_out, lower_out, scale, diag, lower, sems):
    count, width = self_ref.shape[:2]
    scale[pl.ds(0, 8), :] = jnp.zeros((8, width), F32)
    scale[pl.ds(8, count), :] = scale_ref[...].astype(F32)
    lower[0] = jnp.zeros((width, width), BF16)

    def copies(g):
        some = pl.ds(g * group, group)
        return (
            pltpu.make_async_copy(diag.at[some], diag_out.at[some], sems.at[0, g]),
            pltpu.make_async_copy(lower.at[some], lower_out.at[some], sems.at[1, g]),
        )

    def turn(g, carry):
        for i in range(group):
            k = g * group + i
            mine, prev, after = self_ref[k], prev_ref[k], prev_ref[jnp.minimum(k + 1, count - 1)]
            here = scale[pl.ds(k + 8, 1), :].astype(BF16)
            back = scale[pl.ds(k + 7, 1), :].astype(BF16)
            left = jnp.concatenate(
                [
                    jnp.concatenate([mine * here, prev * back], axis=1),
                    jnp.concatenate([after * here, jnp.zeros_like(after)], axis=1),
                ],
                axis=0,
            )
            both = lax.dot_general(left, jnp.concatenate([mine, prev], axis=1), NT, preferred_element_type=F32)
            diag[k] = both[:width].astype(BF16)
            lower[k + 1] = both[width:].astype(BF16)
        for copy in copies(g):
            copy.start()
        return carry

    lax.fori_loop(0, count // group, turn, 0)

    def finish(g, carry):
        for copy in copies(g):
            copy.wait()
        return carry

    lax.fori_loop(0, count // group, finish, 0)


def first_kernel(self_ref, prev_ref, scale_ref, got_ref, diag_in, lower_in, diag_out, lower_out, mine, prev, scale, diag, lower, sems):
    width = mine.shape[1]
    held = [
        pltpu.make_async_copy(self_ref.at[pl.ds(0, 1)], mine, sems.at[0]),
        pltpu.make_async_copy(prev_ref.at[pl.ds(0, 1)], prev, sems.at[1]),
        pltpu.make_async_copy(scale_ref.at[pl.ds(0, 16)], scale, sems.at[2]),
    ]
    for copy in held:
        copy.start()
    for copy in held:
        copy.wait()
    here = scale[...].astype(F32)[0:1].astype(BF16)
    back = got_ref[pl.ds(width, 1), :]
    scaled = prev[0] * back
    left = jnp.concatenate([mine[0] * here, scaled], axis=1)
    right = jnp.concatenate([mine[0], prev[0]], axis=1)
    diag[0] = lax.dot_general(left, right, NT, preferred_element_type=F32).astype(BF16)
    lower[0] = lax.dot_general(scaled, got_ref[pl.ds(0, width), :], NT, preferred_element_type=F32).astype(BF16)
    done = [
        pltpu.make_async_copy(diag, diag_out.at[pl.ds(0, 1)], sems.at[3]),
        pltpu.make_async_copy(lower, lower_out.at[pl.ds(0, 1)], sems.at[4]),
    ]
    for copy in done:
        copy.start()
    for copy in done:
        copy.wait()


def cover(cover_self, cover_prev, scaling):
    count, width = cover_self.shape[:2]
    group = 16
    hbm, vmem = pl.BlockSpec(memory_space=pltpu.HBM), pl.BlockSpec(memory_space=pltpu.VMEM)
    return pl.pallas_call(
        functools.partial(cover_kernel, group),
        out_shape=[jax.ShapeDtypeStruct(cover_self.shape, BF16)] * 2,
        in_specs=[vmem] * 3,
        out_specs=[hbm, hbm],
        scratch_shapes=[
            pltpu.VMEM((8 + count, width), F32),
            pltpu.VMEM(cover_self.shape, BF16),
            pltpu.VMEM((count + 1, width, width), BF16),
            pltpu.SemaphoreType.DMA((2, count // group)),
        ],
        compiler_params=pltpu.CompilerParams(vmem_limit_bytes=16 * 2**20),
        cost_estimate=pl.CostEstimate(
            flops=2 * count * width * 4 * width * width, bytes_accessed=4 * 2 * count * width * width, transcendentals=0
        ),
        name="cover",
    )(cover_self, cover_prev, scaling)


def first_cover(cover_self, cover_prev, scaling, got, diag, lower):
    width = cover_self.shape[1]
    hbm, vmem = pl.BlockSpec(memory_space=pltpu.HBM), pl.BlockSpec(memory_space=pltpu.VMEM)
    block = pltpu.VMEM((1, width, width), BF16)
    cover_self, cover_prev, scaling = (pltpu.with_memory_space_constraint(x, pltpu.HBM) for x in (cover_self, cover_prev, scaling))
    return pl.pallas_call(
        first_kernel,
        out_shape=[jax.ShapeDtypeStruct(x.shape, x.dtype) for x in (diag, lower)],
        in_specs=[hbm, hbm, hbm, vmem, hbm, hbm],
        out_specs=[hbm, hbm],
        input_output_aliases={4: 0, 5: 1},
        scratch_shapes=[block, block, pltpu.VMEM((16, width), BF16), block, block, pltpu.SemaphoreType.DMA((5,))],
        name="first_cover",
    )(cover_self, cover_prev, scaling, got, diag, lower)


def body(capacity_blocks, capacity_rows, cover_self, cover_prev, scaling):
    n_var, n_own, n_sub = (lax.axis_size(a) for a in AXES)
    got = shifted(jnp.concatenate([cover_self[-1], scaling[-1:]], axis=0), AXES, 1)
    side = CAP * capacity_blocks.shape[2]
    ((keep, send),) = capacity(capacity_blocks, capacity_rows, scaling, ((0, side, "own"),))
    total = keep + swap(send, "sub", 1).astype(F32)
    for axis in ("own", "var"):
        arrived = [swap(total[m].astype(BF16), axis, m) for m in send_order(axis)]
        total = functools.reduce(lambda a, b: a + b.astype(F32), arrived, total[0])
        if axis == "own":
            diag, lower = cover(cover_self, cover_prev, scaling)
            total, diag, lower, got = lax.optimization_barrier((total, diag, lower, got))
    diag, lower = first_cover(cover_self, cover_prev, scaling, got, diag, lower)
    return (diag, lower, total)


def solution(mesh):
    split = P(AXES)
    return jax.shard_map(
        body, mesh=mesh, in_specs=(split,) * 5, out_specs=(split,) * 3, check_vma=False
    )
```

profile of v0, /device:TPU:0, one launch (start us, length us, event | category | flops | bytes accessed | tf_op | source)
XLA Modules:
  0.0 46.1 jit_solution(7686160798365765563)
XLA Ops:
  0.6 15.3 %capacity.1 = (f32[4,4,32,1024]{3,2,1,0:T(8,128)S(1)}, bf16[4,4,32,1024]{3,2,1,0:T(8,128)(2,1)S(1)}) custom-call(s32[5,64]{1,0:T(8,128)} %bitcast.31, bf16[64,640,128]{2,1,0:T(8,128)(2,1)} %bitcast.30, bf16[64,128]{1,0:T(8,128)(2,1)} %scale_ref.5), custom_call_target="tpu_custom_call" | custom-call | flops 10737418240 | bytes 14680064 | tf_op jit(solution)/shard_map/capacity/pallas_call | solution.py:125
  16.0 0.5 %collective-permute-start = (bf16[4,4,32,1024]{3,2,1,0:T(8,128)(2,1)S(1)}, bf16[4,4,32,1024]{3,2,1,0:T(8,128)(2,1)S(1)}, u32[]{:S(2)}, u32[]{:S(2)}) collective-permute-start(bf16[4,4,32,1024]{3,2,1,0:T(8,128)(2,1)S(1)} %get-tuple-element.14), channel_id=1, source_target_pairs={{0,1},{1,0},{2,3},{3,2},{4,5},{5,4},{6,7},{7,6},{8,9},{9,8},{10,11... | collective-permute-start | bytes 3145736 | tf_op jit(solution)/shard_map/ppermute | solution.py:18
  16.5 2.3 %collective-permute-done = bf16[4,4,32,1024]{3,2,1,0:T(8,128)(2,1)S(1)} collective-permute-done((bf16[4,4,32,1024]{3,2,1,0:T(8,128)(2,1)S(1)}, bf16[4,4,32,1024]{3,2,1,0:T(8,128)(2,1)S(1)}, u32[]{:S(2)}, u32[]{:S(2)}) %collective-permute-start) | collective-permute-done | bytes 1048608 | tf_op jit(solution)/shard_map/ppermute | solution.py:18
  18.8 0.0 copy-start
  18.8 0.0 copy-start.2
  18.8 0.0 copy-start.1
  18.8 0.4 fusion.5
  19.2 0.1 slice_bitcast_fusion.3
  19.3 3.9 %collective-permute-start.1 = (bf16[4,32,1024]{2,1,0:T(8,128)(2,1)S(1)}, bf16[4,32,1024]{2,1,0:T(8,128)(2,1)S(1)}, u32[]{:S(2)}, u32[]{:S(2)}) collective-permute-start(bf16[4,32,1024]{2,1,0:T(8,128)(2,1)S(1)} %get-tuple-element.25), channel_id=1, source_target_pairs={{0,6},{2,4},{4,2},{6,0},{1,7},{3,5},{5,3},{7,1},{8,14},{10,12},{12... | collective-permute-start | bytes 786440 | tf_op jit(solution)/shard_map/ppermute | solution.py:18
  23.2 0.5 %collective-permute-start.2 = (bf16[4,32,1024]{2,1,0:T(8,128)(2,1)S(1)}, bf16[4,32,1024]{2,1,0:T(8,128)(2,1)S(1)}, u32[]{:S(2)}, u32[]{:S(2)}) collective-permute-start(bf16[4,32,1024]{2,1,0:T(8,128)(2,1)S(1)} %get-tuple-element.27), channel_id=1, source_target_pairs={{0,4},{2,6},{4,0},{6,2},{1,5},{3,7},{5,1},{7,3},{8,12},{10,14},{12... | collective-permute-start | bytes 786440 | tf_op jit(solution)/shard_map/ppermute | solution.py:18
  23.7 0.1 collective-permute-start.3
  23.8 0.0 copy-done
  23.8 0.0 copy-done.2
  23.8 1.5 %collective-permute-start.4 = (bf16[129,128]{1,0:T(8,128)(2,1)S(1)}, bf16[129,128]{1,0:T(8,128)(2,1)S(1)}, u32[]{:S(2)}, u32[]{:S(2)}) collective-permute-start(bf16[129,128]{1,0:T(8,128)(2,1)S(1)} %pad_maximum_fusion), channel_id=1, source_target_pairs={{0,1},{1,2},{2,3},{3,4},{4,5},{5,6},{6,7},{7,8},{8,9},{9,10},{10,1... | collective-permute-start | bytes 99080 | tf_op jit(solution)/shard_map/ppermute | solution.py:23
  25.3 0.0 copy-done.1
  25.3 3.9 %cover.1 = (bf16[64,128,128]{2,1,0:T(8,128)(2,1)}, bf16[64,128,128]{2,1,0:T(8,128)(2,1)}) custom-call(bf16[64,128,128]{2,1,0:T(8,128)(2,1)S(1)} %copy-done, bf16[64,128,128]{2,1,0:T(8,128)(2,1)S(1)} %copy-done.1, bf16[64,128]{1,0:T(8,128)(2,1)S(1)} %copy-done.2), custom_call_target="tpu_custom_call" | custom-call | flops 1073741824 | bytes 8388608 | tf_op jit(solution)/shard_map/cover/pallas_call | solution.py:220
  29.2 1.1 %collective-permute-done.1 = bf16[4,32,1024]{2,1,0:T(8,128)(2,1)S(1)} collective-permute-done((bf16[4,32,1024]{2,1,0:T(8,128)(2,1)S(1)}, bf16[4,32,1024]{2,1,0:T(8,128)(2,1)S(1)}, u32[]{:S(2)}, u32[]{:S(2)}) %collective-permute-start.1) | collective-permute-done | bytes 262176 | tf_op jit(solution)/shard_map/ppermute | solution.py:18
  30.3 5.1 %collective-permute-done.2 = bf16[4,32,1024]{2,1,0:T(8,128)(2,1)S(1)} collective-permute-done((bf16[4,32,1024]{2,1,0:T(8,128)(2,1)S(1)}, bf16[4,32,1024]{2,1,0:T(8,128)(2,1)S(1)}, u32[]{:S(2)}, u32[]{:S(2)}) %collective-permute-start.2) | collective-permute-done | bytes 262176 | tf_op jit(solution)/shard_map/ppermute | solution.py:18
  35.4 0.7 %collective-permute-done.3 = bf16[4,32,1024]{2,1,0:T(8,128)(2,1)S(1)} collective-permute-done((bf16[4,32,1024]{2,1,0:T(8,128)(2,1)S(1)}, bf16[4,32,1024]{2,1,0:T(8,128)(2,1)S(1)}, u32[]{:S(2)}, u32[]{:S(2)}) %collective-permute-start.3) | collective-permute-done | bytes 262176 | tf_op jit(solution)/shard_map/ppermute | solution.py:18
  36.1 0.1 fusion.2
  36.2 0.0 collective-permute-done.4.got_ref
  36.2 0.0 copy-start.3
  36.3 2.7 %collective-permute-start.5 = (bf16[32,1024]{1,0:T(8,128)(2,1)S(1)}, bf16[32,1024]{1,0:T(8,128)(2,1)S(1)}, u32[]{:S(2)}, u32[]{:S(2)}) collective-permute-start(bf16[32,1024]{1,0:T(8,128)(2,1)S(1)} %get-tuple-element.28), channel_id=1, source_target_pairs={{0,16},{8,24},{16,0},{24,8},{1,17},{9,25},{17,1},{25,9},{2,18},{10... | collective-permute-start | bytes 196616 | tf_op jit(solution)/shard_map/ppermute | solution.py:18
  38.9 1.3 %collective-permute-start.6 = (bf16[32,1024]{1,0:T(8,128)(2,1)S(1)}, bf16[32,1024]{1,0:T(8,128)(2,1)S(1)}, u32[]{:S(2)}, u32[]{:S(2)}) collective-permute-start(bf16[32,1024]{1,0:T(8,128)(2,1)S(1)} %get-tuple-element.30), channel_id=1, source_target_pairs={{0,24},{8,16},{16,8},{24,0},{1,25},{9,17},{17,9},{25,1},{2,26},{10... | collective-permute-start | bytes 196616 | tf_op jit(solution)/shard_map/ppermute | solution.py:18
  40.3 0.2 collective-permute-start.7
  40.5 0.0 copy-done.3
  40.5 2.4 %first_cover.1 = (bf16[64,128,128]{2,1,0:T(8,128)(2,1)}, bf16[64,128,128]{2,1,0:T(8,128)(2,1)}) custom-call(bf16[64,128,128]{2,1,0:T(8,128)(2,1)} %self_ref.3, bf16[64,128,128]{2,1,0:T(8,128)(2,1)} %prev_ref.3, bf16[64,128]{1,0:T(8,128)(2,1)} %scale_ref.5, bf16[129,128]{1,0:T(8,128)(2,1)} %copy-done.3, ...), custom_call_target="tpu_custom_call", output_to_operand_aliasing={{0}: (4, {}), {1}: (5, {})} | custom-call | tf_op jit(solution)/shard_map/first_cover/pallas_call | solution.py:244
  42.9 1.0 %collective-permute-done.5 = bf16[32,1024]{1,0:T(8,128)(2,1)S(1)} collective-permute-done((bf16[32,1024]{1,0:T(8,128)(2,1)S(1)}, bf16[32,1024]{1,0:T(8,128)(2,1)S(1)}, u32[]{:S(2)}, u32[]{:S(2)}) %collective-permute-start.5) | collective-permute-done | bytes 65568 | tf_op jit(solution)/shard_map/ppermute | solution.py:18
  43.9 1.3 %collective-permute-done.6 = bf16[32,1024]{1,0:T(8,128)(2,1)S(1)} collective-permute-done((bf16[32,1024]{1,0:T(8,128)(2,1)S(1)}, bf16[32,1024]{1,0:T(8,128)(2,1)S(1)}, u32[]{:S(2)}, u32[]{:S(2)}) %collective-permute-start.6) | collective-permute-done | bytes 65568 | tf_op jit(solution)/shard_map/ppermute | solution.py:18
  45.2 0.2 collective-permute-done.7
  45.4 0.7 %fusion.4 = f32[32,1024]{1,0:T(8,128)} fusion(bf16[32,1024]{1,0:T(8,128)(2,1)S(1)} %collective-permute-done.7, bf16[32,1024]{1,0:T(8,128)(2,1)S(1)} %collective-permute-done.6, bf16[32,1024]{1,0:T(8,128)(2,1)S(1)} %collective-permute-done.5, f32[4,32,1024]{2,1,0:T(8,128)S(1)} %fusion.2), kind=kLoop, calls=%fused_computation.10 | loop fusion | flops 196608 | bytes 458752 | tf_op jit(solution)/shard_map/add | solution.py:263
  (5 shorter events, 0.1 us)
Async XLA Ops:
  16.0 2.8 %collective-permute-start = (bf16[4,4,32,1024]{3,2,1,0:T(8,128)(2,1)S(1)}, bf16[4,4,32,1024]{3,2,1,0:T(8,128)(2,1)S(1)}, u32[]{:S(2)}, u32[]{:S(2)}) collective-permute-start(bf16[4,4,32,1024]{3,2,1,0:T(8,128)(2,1)S(1)} %get-tuple-element.14), channel_id=1, source_target_pairs={{0,1},{1,0},{2,3},{3,2},{4,5},{5,4},{6,7},{7,6},{8,9},{9,8},{10,11... | collective-permute-start | bytes 3145736 | tf_op jit(solution)/shard_map/ppermute | solution.py:18
  18.8 5.0 %copy-start = (bf16[64,128,128]{2,1,0:T(8,128)(2,1)S(1)}, bf16[64,128,128]{2,1,0:T(8,128)(2,1)}, u32[]{:S(2)}) copy-start(bf16[64,128,128]{2,1,0:T(8,128)(2,1)} %self_ref.3) | copy-start | bytes 6291460
  18.8 5.1 %copy-start.2 = (bf16[64,128]{1,0:T(8,128)(2,1)S(1)}, bf16[64,128]{1,0:T(8,128)(2,1)}, u32[]{:S(2)}) copy-start(bf16[64,128]{1,0:T(8,128)(2,1)} %scale_ref.5) | copy-start | bytes 49156
  18.8 6.6 %copy-start.1 = (bf16[64,128,128]{2,1,0:T(8,128)(2,1)S(1)}, bf16[64,128,128]{2,1,0:T(8,128)(2,1)}, u32[]{:S(2)}) copy-start(bf16[64,128,128]{2,1,0:T(8,128)(2,1)} %prev_ref.3) | copy-start | bytes 6291460
  19.3 11.0 %collective-permute-start.1 = (bf16[4,32,1024]{2,1,0:T(8,128)(2,1)S(1)}, bf16[4,32,1024]{2,1,0:T(8,128)(2,1)S(1)}, u32[]{:S(2)}, u32[]{:S(2)}) collective-permute-start(bf16[4,32,1024]{2,1,0:T(8,128)(2,1)S(1)} %get-tuple-element.25), channel_id=1, source_target_pairs={{0,6},{2,4},{4,2},{6,0},{1,7},{3,5},{5,3},{7,1},{8,14},{10,12},{12... | collective-permute-start | bytes 786440 | tf_op jit(solution)/shard_map/ppermute | solution.py:18
  23.2 12.2 %collective-permute-start.2 = (bf16[4,32,1024]{2,1,0:T(8,128)(2,1)S(1)}, bf16[4,32,1024]{2,1,0:T(8,128)(2,1)S(1)}, u32[]{:S(2)}, u32[]{:S(2)}) collective-permute-start(bf16[4,32,1024]{2,1,0:T(8,128)(2,1)S(1)} %get-tuple-element.27), channel_id=1, source_target_pairs={{0,4},{2,6},{4,0},{6,2},{1,5},{3,7},{5,1},{7,3},{8,12},{10,14},{12... | collective-permute-start | bytes 786440 | tf_op jit(solution)/shard_map/ppermute | solution.py:18
  23.7 12.4 %collective-permute-start.3 = (bf16[4,32,1024]{2,1,0:T(8,128)(2,1)S(1)}, bf16[4,32,1024]{2,1,0:T(8,128)(2,1)S(1)}, u32[]{:S(2)}, u32[]{:S(2)}) collective-permute-start(bf16[4,32,1024]{2,1,0:T(8,128)(2,1)S(1)} %get-tuple-element.26), channel_id=1, source_target_pairs={{0,2},{2,0},{4,6},{6,4},{1,3},{3,1},{5,7},{7,5},{8,10},{10,8},{12,... | collective-permute-start | bytes 786440 | tf_op jit(solution)/shard_map/ppermute | solution.py:18
  23.8 12.4 %collective-permute-start.4 = (bf16[129,128]{1,0:T(8,128)(2,1)S(1)}, bf16[129,128]{1,0:T(8,128)(2,1)S(1)}, u32[]{:S(2)}, u32[]{:S(2)}) collective-permute-start(bf16[129,128]{1,0:T(8,128)(2,1)S(1)} %pad_maximum_fusion), channel_id=1, source_target_pairs={{0,1},{1,2},{2,3},{3,4},{4,5},{5,6},{6,7},{7,8},{8,9},{9,10},{10,1... | collective-permute-start | bytes 99080 | tf_op jit(solution)/shard_map/ppermute | solution.py:23
  36.2 4.3 %copy-start.3 = (bf16[129,128]{1,0:T(8,128)(2,1)}, bf16[129,128]{1,0:T(8,128)(2,1)S(1)}, u32[]{:S(2)}) copy-start(bf16[129,128]{1,0:T(8,128)(2,1)S(1)} %collective-permute-done.4.got_ref) | copy-start | bytes 99076
  36.3 7.6 %collective-permute-start.5 = (bf16[32,1024]{1,0:T(8,128)(2,1)S(1)}, bf16[32,1024]{1,0:T(8,128)(2,1)S(1)}, u32[]{:S(2)}, u32[]{:S(2)}) collective-permute-start(bf16[32,1024]{1,0:T(8,128)(2,1)S(1)} %get-tuple-element.28), channel_id=1, source_target_pairs={{0,16},{8,24},{16,0},{24,8},{1,17},{9,25},{17,1},{25,9},{2,18},{10... | collective-permute-start | bytes 196616 | tf_op jit(solution)/shard_map/ppermute | solution.py:18
  38.9 6.3 %collective-permute-start.6 = (bf16[32,1024]{1,0:T(8,128)(2,1)S(1)}, bf16[32,1024]{1,0:T(8,128)(2,1)S(1)}, u32[]{:S(2)}, u32[]{:S(2)}) collective-permute-start(bf16[32,1024]{1,0:T(8,128)(2,1)S(1)} %get-tuple-element.30), channel_id=1, source_target_pairs={{0,24},{8,16},{16,8},{24,0},{1,25},{9,17},{17,9},{25,1},{2,26},{10... | collective-permute-start | bytes 196616 | tf_op jit(solution)/shard_map/ppermute | solution.py:18
  40.3 5.1 %collective-permute-start.7 = (bf16[32,1024]{1,0:T(8,128)(2,1)S(1)}, bf16[32,1024]{1,0:T(8,128)(2,1)S(1)}, u32[]{:S(2)}, u32[]{:S(2)}) collective-permute-start(bf16[32,1024]{1,0:T(8,128)(2,1)S(1)} %get-tuple-element.29), channel_id=1, source_target_pairs={{0,8},{8,0},{16,24},{24,16},{1,9},{9,1},{17,25},{25,17},{2,10},{10... | collective-permute-start | bytes 196616 | tf_op jit(solution)/shard_map/ppermute | solution.py:18
where the time goes:
time: 46.4 us; the launch traced here: 46.1 us
  Pallas kernels  21.6 us (47%)
  waiting for transfers between devices  11.6 us (25%)
  starting transfers between devices  10.8 us (23%)
  other arithmetic  1.32 us (3%)
  between operations  0.75 us (2%)
    pallas_call x1, Pallas kernels, capacity(): pl.pallas_call(functools.partial(capacity_kernel, step, parts, (n_var, n_...  15.3 us
    ppermute x7, waiting for transfers between devices, swap(): return lax.ppermute(value, axis, [(i, i ^ mask) for i in range(count)])  11.6 us
    ppermute x7, starting transfers between devices, swap(): return lax.ppermute(value, axis, [(i, i ^ mask) for i in range(count)])  9.28 us
    pallas_call x1, Pallas kernels, cover(): pl.pallas_call(functools.partial(cover_kernel, group), out_shape=[jax.Sha...  3.87 us
    pallas_call x1, Pallas kernels, first_cover(): pl.pallas_call(first_kernel, out_shape=[jax.ShapeDtypeStruct(x.shape, x.d...  2.39 us
    ppermute x1, starting transfers between devices, shifted(): lax.ppermute(value, axis, [(i, i + steps) for i in range(count - steps)])  1.48 us
  transfers between devices with their start and end apart: 8, of which 7 were waited for; matrix products, arithmetic and copies ran while one was open for 0% of the time, Pallas kernels for 14%

commit v1 on v0

--- a/solution.py
+++ b/solution.py
@@ -37,12 +37,36 @@
     return found
 
 
-def capacity_kernel(step, parts, sizes, rows_ref, cap_ref, scale_ref, *rest):
-    outs, (dense, scale_in, scale, acc, sems, scale_sem) = rest[: 2 * len(parts)], rest[2 * len(parts) :]
+def multiply(dense, scale, acc, ks, low, tile):
+    side = dense.shape[1]
+    for j in range(low, low + acc.shape[1] // tile):
+        right = jnp.concatenate(
+            [dense[k, pl.ds(tile * j, tile), :] * scale[pl.ds(k, 1), :].astype(BF16) for k in ks], axis=1
+        )
+        under = pl.ds(tile * j, side - tile * j)
+        left = jnp.concatenate([dense[k, under, :] for k in ks], axis=1)
+        acc[under, pl.ds(tile * (j - low), tile)] += lax.dot_general(left, right, NT, preferred_element_type=F32)
+
+
+def emit(acc, keep_ref, send_ref, order):
+    var, own, sub = (lax.axis_index(a) for a in AXES)
+    n_var, n_own = (keep_ref.shape[1], keep_ref.shape[0]) if order == "own" else keep_ref.shape[:2]
+    held = keep_ref.shape[2]
+    for m in range(n_own):
+
+        def one(v, carry, m=m):
+            chip = (var ^ v) * n_own + (own ^ m)
+            slot = (m, v) if order == "own" else (v, m)
+            keep_ref[slot] = acc[pl.ds(pl.multiple_of((2 * chip + sub) * held, held), held), :]
+            send_ref[slot] = acc[pl.ds(pl.multiple_of((2 * chip + 1 - sub) * held, held), held), :].astype(send_ref.dtype)
+            return carry
+
+        lax.fori_loop(0, n_var, one, 0, unroll=True)
+
+
+def left_kernel(step, order, rows_ref, cap_ref, scale_ref, dense, scale, acc, keep_ref, send_ref, scale_in, sems, scale_sem):
     count, width = cap_ref.shape[0], cap_ref.shape[2]
     nz = cap_ref.shape[1] // width
-    turns = count // step
-    side = acc.shape[0]
     tile = 2 * width
 
     def spot(r):
@@ -74,72 +98,78 @@
             dense.at[pl.ds(first, step), pl.ds(0, nz * width), :],
             sems.at[t],
         ).wait()
-        ks = [first + i for i in range(step)]
-        for j in range(side // tile):
-            right = jnp.concatenate(
-                [dense[k, pl.ds(tile * j, tile), :] * scale[pl.ds(k, 1), :].astype(BF16) for k in ks], axis=1
-            )
-            left = jnp.concatenate([dense[k, pl.ds(0, tile * (j + 1)), :] for k in ks], axis=1)
-            acc[pl.ds(0, tile * (j + 1)), pl.ds(tile * j, tile)] += lax.dot_general(
-                left, right, NT, preferred_element_type=F32
-            )
-        return carry
-
-    lax.fori_loop(0, turns, turn, 0)
-    for i in range(side // tile):
-        for j in range(i):
+        multiply(dense, scale, acc, [first + i for i in range(step)], 0, tile)
+        return carry
+
+    lax.fori_loop(0, count // step, turn, 0)
+    for j in range(acc.shape[1] // tile):
+        for i in range(j):
             acc[pl.ds(tile * i, tile), pl.ds(tile * j, tile)] = acc[pl.ds(tile * j, tile), pl.ds(tile * i, tile)].T
-    var, own, sub = (lax.axis_index(a) for a in AXES)
-    n_var, n_own, held = sizes
-    for at, (low, high, first) in enumerate(parts):
-        keep_ref, send_ref = outs[2 * at], outs[2 * at + 1]
-        for m in range(n_own):
-
-            def emit(v, carry, m=m):
-                chip = (var ^ v) * n_own + (own ^ m)
-                mine = pl.ds(pl.multiple_of((2 * chip + sub) * held, held), held)
-                other = pl.ds(pl.multiple_of((2 * chip + 1 - sub) * held, held), held)
-                slot = (m, v) if first == "own" else (v, m)
-                keep_ref[slot] = acc[mine, pl.ds(low, high - low)]
-                send_ref[slot] = acc[other, pl.ds(low, high - low)].astype(send_ref.dtype)
-                return carry
-
-            lax.fori_loop(0, n_var, emit, 0, unroll=True)
-
-
-def capacity(capacity_blocks, capacity_rows, scaling, parts):
+    emit(acc, keep_ref, send_ref, order)
+
+
+def right_kernel(step, order, dense, scale, before, keep_ref, send_ref, acc):
+    count, tile = dense.shape[0], 2 * dense.shape[2]
+    low = before.shape[1] // tile
+    acc[...] = jnp.zeros_like(acc)
+
+    def turn(t, carry):
+        multiply(dense, scale, acc, [t * step + i for i in range(step)], low, tile)
+        return carry
+
+    lax.fori_loop(0, count // step, turn, 0)
+    for j in range(low, low + acc.shape[1] // tile):
+        for i in range(j):
+            source, at = (before, i) if i < low else (acc, i - low)
+            acc[pl.ds(tile * i, tile), pl.ds(tile * (j - low), tile)] = source[pl.ds(tile * j, tile), pl.ds(tile * at, tile)].T
+    emit(acc, keep_ref, send_ref, order)
+
+
+def capacity(capacity_blocks, capacity_rows, scaling, cut, orders):
     count, nz, width = capacity_blocks.shape[:3]
     n_var, n_own, n_sub = (lax.axis_size(a) for a in AXES)
     side = CAP * width
     held = side // (n_var * n_own * n_sub)
     step = 32
     sent = BF16 if held % 16 == 0 else F32
-    shapes = []
-    for low, high, first in parts:
-        lead = (n_own, n_var) if first == "own" else (n_var, n_own)
-        shapes += [jax.ShapeDtypeStruct(lead + (held, high - low), t) for t in (F32, sent)]
+
+    def shapes(columns, order):
+        lead = (n_own, n_var) if order == "own" else (n_var, n_own)
+        return [jax.ShapeDtypeStruct(lead + (held, columns), t) for t in (F32, sent)]
+
     hbm = pl.BlockSpec(memory_space=pltpu.HBM)
     smem, vmem = pl.BlockSpec(memory_space=pltpu.SMEM), pl.BlockSpec(memory_space=pltpu.VMEM)
     operands = (capacity_rows.T, capacity_blocks.reshape(count, nz * width, width), scaling)
-    flops = 2 * side * side * count * width * 5 // 8
-    outs = pl.pallas_call(
-        functools.partial(capacity_kernel, step, parts, (n_var, n_own, held)),
-        out_shape=shapes,
+    dense, scale, left, *first = pl.pallas_call(
+        functools.partial(left_kernel, step, orders[0]),
+        out_shape=[
+            pltpu.VMEM((count, side, width), BF16),
+            pltpu.VMEM((count, width), F32),
+            pltpu.VMEM((side, cut), F32),
+            *shapes(cut, orders[0]),
+        ],
         in_specs=[smem, hbm, hbm],
-        out_specs=[vmem] * len(shapes),
+        out_specs=[vmem] * 5,
         scratch_shapes=[
-            pltpu.VMEM((count, side, width), BF16),
             pltpu.VMEM((count, width), BF16),
-            pltpu.VMEM((count, width), F32),
-            pltpu.VMEM((side, side), F32),
             pltpu.SemaphoreType.DMA((count // step,)),
             pltpu.SemaphoreType.DMA,
         ],
-        compiler_params=pltpu.CompilerParams(vmem_limit_bytes=32 * 2**20),
-        cost_estimate=pl.CostEstimate(flops=flops, bytes_accessed=14 * 2**20, transcendentals=0),
-        name="capacity",
+        compiler_params=pltpu.CompilerParams(vmem_limit_bytes=30 * 2**20),
+        cost_estimate=pl.CostEstimate(flops=2 * side * cut * count * width, bytes_accessed=14 * 2**20, transcendentals=0),
+        name="capacity_left",
     )(*(pltpu.with_memory_space_constraint(x, pltpu.HBM) for x in operands))
-    return [(keep, send.astype(BF16)) for keep, send in zip(outs[0::2], outs[1::2])]
+    second = pl.pallas_call(
+        functools.partial(right_kernel, step, orders[1]),
+        out_shape=shapes(side - cut, orders[1]),
+        in_specs=[vmem] * 3,
+        out_specs=[vmem] * 2,
+        scratch_shapes=[pltpu.VMEM((side, side - cut), F32)],
+        compiler_params=pltpu.CompilerParams(vmem_limit_bytes=30 * 2**20),
+        cost_estimate=pl.CostEstimate(flops=2 * side * cut * count * width, bytes_accessed=2**20, transcendentals=0),
+        name="capacity_right",
+    )(*(pltpu.with_memory_space_constraint(x, pltpu.VMEM) for x in (dense, scale, left)))
+    return [(keep, send.astype(BF16)) for keep, send in (first, second)]
 
 
 def cover_kernel(group, self_ref, prev_ref, scale_ref, diag_out, lower_out, scale, diag, lower, sems):
@@ -254,15 +284,18 @@
 
 def body(capacity_blocks, capacity_rows, cover_self, cover_prev, scaling):
     n_var, n_own, n_sub = (lax.axis_size(a) for a in AXES)
-    got = shifted(jnp.concatenate([cover_self[-1], scaling[-1:]], axis=0), AXES, 1)
+    tail = jnp.concatenate([cover_self[-1], scaling[-1:]], axis=0)
     side = CAP * capacity_blocks.shape[2]
-    ((keep, send),) = capacity(capacity_blocks, capacity_rows, scaling, ((0, side, "own"),))
-    total = keep + swap(send, "sub", 1).astype(F32)
+    sums = capacity(capacity_blocks, capacity_rows, scaling, side // 4 * 3, ("own", "own"))
+    received = [swap(send, "sub", 1) for _, send in sums]
+    received, tail, covered = lax.optimization_barrier((received, tail, (cover_self, cover_prev, scaling)))
+    total = jnp.concatenate([keep + term.astype(F32) for (keep, _), term in zip(sums, received)], axis=-1)
+    got = shifted(tail, AXES, 1)
     for axis in ("own", "var"):
         arrived = [swap(total[m].astype(BF16), axis, m) for m in send_order(axis)]
         total = functools.reduce(lambda a, b: a + b.astype(F32), arrived, total[0])
         if axis == "own":
-            diag, lower = cover(cover_self, cover_prev, scaling)
+            diag, lower = cover(*covered)
             total, diag, lower, got = lax.optimization_barrier((total, diag, lower, got))
     diag, lower = first_cover(cover_self, cover_prev, scaling, got, diag, lower)
     return (diag, lower, total)

time: 46.4 us -> 46.2 us (level)
  waiting for transfers between devices: 11.6 us -> 10.8 us
  Pallas kernels: 21.6 us -> 22.1 us
    ppermute x7 -> x8, waiting for transfers between devices: 11.6 us -> 10.8 us  [swap(): return lax.ppermute(value, axis, [(i, i ^ mask) for i in range(count)])]
    pallas_call x1 -> x2, Pallas kernels: 15.3 us -> 15.8 us  [the longest x1 13.9 us: capacity(): pl.pallas_call(functools.partial(left_kernel, step, orders[0]), out_shape...]
    ppermute x7 -> x8, starting transfers between devices: 9.28 us -> 9.17 us  [swap(): return lax.ppermute(value, axis, [(i, i ^ mask) for i in range(count)])]
  transfers between devices with their start and end apart: 8 -> 9, of which waited for: 7 -> 7; matrix products, arithmetic and copies ran while one was open for 0% -> 0% of each run, Pallas kernels for 14% -> 18%
where the time goes in v1:
time: 46.2 us; the launch traced here: 45.9 us
  Pallas kernels  22.1 us (48%)
  starting transfers between devices  10.9 us (24%)
  waiting for transfers between devices  10.8 us (23%)
  other arithmetic  1.25 us (3%)
  between operations  0.78 us (2%)
    pallas_call x1, Pallas kernels, capacity(): pl.pallas_call(functools.partial(left_kernel, step, orders[0]), out_shape...  13.9 us
    ppermute x8, waiting for transfers between devices, swap(): return lax.ppermute(value, axis, [(i, i ^ mask) for i in range(count)])  10.8 us
    ppermute x8, starting transfers between devices, swap(): return lax.ppermute(value, axis, [(i, i ^ mask) for i in range(count)])  9.17 us
    pallas_call x1, Pallas kernels, cover(): pl.pallas_call(functools.partial(cover_kernel, group), out_shape=[jax.Sha...  3.87 us
    pallas_call x1, Pallas kernels, first_cover(): pl.pallas_call(first_kernel, out_shape=[jax.ShapeDtypeStruct(x.shape, x.d...  2.39 us
    pallas_call x1, Pallas kernels, capacity(): pl.pallas_call(functools.partial(right_kernel, step, orders[1]), out_shap...  1.89 us
    ppermute x1, starting transfers between devices, shifted(): lax.ppermute(value, axis, [(i, i + steps) for i in range(count - steps)])  1.69 us
  transfers between devices with their start and end apart: 9, of which 7 were waited for; matrix products, arithmetic and copies ran while one was open for 0% of the time, Pallas kernels for 18%

profile of v1, /device:TPU:0, one launch (start us, length us, event | category | flops | bytes accessed | tf_op | source)
XLA Modules:
  0.0 45.9 jit_solution(3534909490250297468)
XLA Ops:
  0.6 13.9 %capacity_left.1 = (bf16[64,1024,128]{2,1,0:T(8,128)(2,1)S(1)}, f32[64,128]{1,0:T(8,128)S(1)}, f32[1024,768]{1,0:T(8,128)S(1)}, f32[4,4,32,768]{3,2,1,0:T(8,128)S(1)}, bf16[4,4,32,768]{3,2,1,0:T(8,128)(2,1)S(1)}) custom-call(s32[5,64]{1,0:T(8,128)} %bitcast.31, bf16[64,640,128]{2,1,0:T(8,128)(2,1)} %bitcast.30, bf16[64,128]{1,0:T(8,128)(2,1)} %scale_ref.4), custom_call_target="tpu_custom_call" | custom-call | flops 12884901888 | bytes 14680064 | tf_op jit(solution)/shard_map/capacity_left/pallas_call | solution.py:143
  14.6 0.5 %collective-permute-start = (bf16[4,4,32,768]{3,2,1,0:T(8,128)(2,1)S(1)}, bf16[4,4,32,768]{3,2,1,0:T(8,128)(2,1)S(1)}, u32[]{:S(2)}, u32[]{:S(2)}) collective-permute-start(bf16[4,4,32,768]{3,2,1,0:T(8,128)(2,1)S(1)} %get-tuple-element.25), channel_id=1, source_target_pairs={{0,1},{1,0},{2,3},{3,2},{4,5},{5,4},{6,7},{7,6},{8,9},{9,8},{10,11... | collective-permute-start | bytes 2359304 | tf_op jit(solution)/shard_map/ppermute | solution.py:18
  15.1 0.0 copy-start.2
  15.1 0.0 copy-start
  15.1 1.9 %capacity_right.1 = (f32[4,4,32,256]{3,2,1,0:T(8,128)S(1)}, bf16[4,4,32,256]{3,2,1,0:T(8,128)(2,1)S(1)}) custom-call(bf16[64,1024,128]{2,1,0:T(8,128)(2,1)S(1)} %get-tuple-element.26.dense, f32[64,128]{1,0:T(8,128)S(1)} %get-tuple-element.27.scale, f32[1024,768]{1,0:T(8,128)S(1)} %get-tuple-element.28.before), custom_call_target="tpu_custom_call" | custom-call | flops 12884901888 | bytes 1048576 | tf_op jit(solution)/shard_map/capacity_right/pallas_call | solution.py:162
  17.0 0.1 collective-permute-start.1
  17.1 0.0 copy-done.2
  17.1 0.0 copy-done
  17.2 1.4 %collective-permute-done.1 = bf16[4,4,32,256]{3,2,1,0:T(8,128)(2,1)S(1)} collective-permute-done((bf16[4,4,32,256]{3,2,1,0:T(8,128)(2,1)S(1)}, bf16[4,4,32,256]{3,2,1,0:T(8,128)(2,1)S(1)}, u32[]{:S(2)}, u32[]{:S(2)}) %collective-permute-start.1) | collective-permute-done | bytes 262176 | tf_op jit(solution)/shard_map/ppermute | solution.py:18
  18.6 0.0 collective-permute-done
  18.6 0.1 convert_add_fusion.1
  18.7 0.2 convert_add_fusion
  18.9 0.0 copy-start.1
  18.9 0.2 fusion
  19.0 0.1 slice_bitcast_fusion.2
  19.1 3.7 %collective-permute-start.2 = (bf16[4,32,1024]{2,1,0:T(8,128)(2,1)S(1)}, bf16[4,32,1024]{2,1,0:T(8,128)(2,1)S(1)}, u32[]{:S(2)}, u32[]{:S(2)}) collective-permute-start(bf16[4,32,1024]{2,1,0:T(8,128)(2,1)S(1)} %get-tuple-element.45), channel_id=1, source_target_pairs={{0,6},{2,4},{4,2},{6,0},{1,7},{3,5},{5,3},{7,1},{8,14},{10,12},{12... | collective-permute-start | bytes 786440 | tf_op jit(solution)/shard_map/ppermute | solution.py:18
  22.8 0.5 %collective-permute-start.3 = (bf16[4,32,1024]{2,1,0:T(8,128)(2,1)S(1)}, bf16[4,32,1024]{2,1,0:T(8,128)(2,1)S(1)}, u32[]{:S(2)}, u32[]{:S(2)}) collective-permute-start(bf16[4,32,1024]{2,1,0:T(8,128)(2,1)S(1)} %get-tuple-element.47), channel_id=1, source_target_pairs={{0,4},{2,6},{4,0},{6,2},{1,5},{3,7},{5,1},{7,3},{8,12},{10,14},{12... | collective-permute-start | bytes 786440 | tf_op jit(solution)/shard_map/ppermute | solution.py:18
  23.3 0.1 collective-permute-start.4
  23.4 1.7 %collective-permute-start.5 = (bf16[129,128]{1,0:T(8,128)(2,1)S(1)}, bf16[129,128]{1,0:T(8,128)(2,1)S(1)}, u32[]{:S(2)}, u32[]{:S(2)}) collective-permute-start(bf16[129,128]{1,0:T(8,128)(2,1)S(1)} %pad_maximum_fusion.1), channel_id=1, source_target_pairs={{0,1},{1,2},{2,3},{3,4},{4,5},{5,6},{6,7},{7,8},{8,9},{9,10},{10,1... | collective-permute-start | bytes 99080 | tf_op jit(solution)/shard_map/ppermute | solution.py:23
  25.1 0.0 copy-done.1
  25.1 3.9 %cover.1 = (bf16[64,128,128]{2,1,0:T(8,128)(2,1)}, bf16[64,128,128]{2,1,0:T(8,128)(2,1)}) custom-call(bf16[64,128,128]{2,1,0:T(8,128)(2,1)S(1)} %copy-done, bf16[64,128,128]{2,1,0:T(8,128)(2,1)S(1)} %copy-done.1, bf16[64,128]{1,0:T(8,128)(2,1)S(1)} %copy-done.2), custom_call_target="tpu_custom_call" | custom-call | flops 1073741824 | bytes 8388608 | tf_op jit(solution)/shard_map/cover/pallas_call | solution.py:250
  29.0 1.0 %collective-permute-done.2 = bf16[4,32,1024]{2,1,0:T(8,128)(2,1)S(1)} collective-permute-done((bf16[4,32,1024]{2,1,0:T(8,128)(2,1)S(1)}, bf16[4,32,1024]{2,1,0:T(8,128)(2,1)S(1)}, u32[]{:S(2)}, u32[]{:S(2)}) %collective-permute-start.2) | collective-permute-done | bytes 262176 | tf_op jit(solution)/shard_map/ppermute | solution.py:18
  29.9 5.3 %collective-permute-done.3 = bf16[4,32,1024]{2,1,0:T(8,128)(2,1)S(1)} collective-permute-done((bf16[4,32,1024]{2,1,0:T(8,128)(2,1)S(1)}, bf16[4,32,1024]{2,1,0:T(8,128)(2,1)S(1)}, u32[]{:S(2)}, u32[]{:S(2)}) %collective-permute-start.3) | collective-permute-done | bytes 262176 | tf_op jit(solution)/shard_map/ppermute | solution.py:18
  35.2 0.7 %collective-permute-done.4 = bf16[4,32,1024]{2,1,0:T(8,128)(2,1)S(1)} collective-permute-done((bf16[4,32,1024]{2,1,0:T(8,128)(2,1)S(1)}, bf16[4,32,1024]{2,1,0:T(8,128)(2,1)S(1)}, u32[]{:S(2)}, u32[]{:S(2)}) %collective-permute-start.4) | collective-permute-done | bytes 262176 | tf_op jit(solution)/shard_map/ppermute | solution.py:18
  35.9 0.1 fusion.5
  36.0 0.0 collective-permute-done.5.got_ref
  36.0 0.0 copy-start.3
  36.1 2.7 %collective-permute-start.6 = (bf16[32,1024]{1,0:T(8,128)(2,1)S(1)}, bf16[32,1024]{1,0:T(8,128)(2,1)S(1)}, u32[]{:S(2)}, u32[]{:S(2)}) collective-permute-start(bf16[32,1024]{1,0:T(8,128)(2,1)S(1)} %get-tuple-element.48), channel_id=1, source_target_pairs={{0,16},{8,24},{16,0},{24,8},{1,17},{9,25},{17,1},{25,9},{2,18},{10... | collective-permute-start | bytes 196616 | tf_op jit(solution)/shard_map/ppermute | solution.py:18
  38.8 1.3 %collective-permute-start.7 = (bf16[32,1024]{1,0:T(8,128)(2,1)S(1)}, bf16[32,1024]{1,0:T(8,128)(2,1)S(1)}, u32[]{:S(2)}, u32[]{:S(2)}) collective-permute-start(bf16[32,1024]{1,0:T(8,128)(2,1)S(1)} %get-tuple-element.50), channel_id=1, source_target_pairs={{0,24},{8,16},{16,8},{24,0},{1,25},{9,17},{17,9},{25,1},{2,26},{10... | collective-permute-start | bytes 196616 | tf_op jit(solution)/shard_map/ppermute | solution.py:18
  40.1 0.2 collective-permute-start.8
  40.3 0.0 copy-done.3
  40.3 2.4 %first_cover.1 = (bf16[64,128,128]{2,1,0:T(8,128)(2,1)}, bf16[64,128,128]{2,1,0:T(8,128)(2,1)}) custom-call(bf16[64,128,128]{2,1,0:T(8,128)(2,1)} %self_ref.2, bf16[64,128,128]{2,1,0:T(8,128)(2,1)} %prev_ref.2, bf16[64,128]{1,0:T(8,128)(2,1)} %scale_ref.4, bf16[129,128]{1,0:T(8,128)(2,1)} %copy-done.3, ...), custom_call_target="tpu_custom_call", output_to_operand_aliasing={{0}: (4, {}), {1}: (5, {})} | custom-call | tf_op jit(solution)/shard_map/first_cover/pallas_call | solution.py:274
  42.7 1.0 %collective-permute-done.6 = bf16[32,1024]{1,0:T(8,128)(2,1)S(1)} collective-permute-done((bf16[32,1024]{1,0:T(8,128)(2,1)S(1)}, bf16[32,1024]{1,0:T(8,128)(2,1)S(1)}, u32[]{:S(2)}, u32[]{:S(2)}) %collective-permute-start.6) | collective-permute-done | bytes 65568 | tf_op jit(solution)/shard_map/ppermute | solution.py:18
  43.8 1.3 %collective-permute-done.7 = bf16[32,1024]{1,0:T(8,128)(2,1)S(1)} collective-permute-done((bf16[32,1024]{1,0:T(8,128)(2,1)S(1)}, bf16[32,1024]{1,0:T(8,128)(2,1)S(1)}, u32[]{:S(2)}, u32[]{:S(2)}) %collective-permute-start.7) | collective-permute-done | bytes 65568 | tf_op jit(solution)/shard_map/ppermute | solution.py:18
  45.1 0.2 collective-permute-done.8
  45.3 0.7 %fusion.7 = f32[32,1024]{1,0:T(8,128)} fusion(bf16[32,1024]{1,0:T(8,128)(2,1)S(1)} %collective-permute-done.8, bf16[32,1024]{1,0:T(8,128)(2,1)S(1)} %collective-permute-done.7, bf16[32,1024]{1,0:T(8,128)(2,1)S(1)} %collective-permute-done.6, f32[4,32,1024]{2,1,0:T(8,128)S(1)} %fusion.5), kind=kLoop, calls=%fused_computation.16 | loop fusion | flops 196608 | bytes 458752 | tf_op jit(solution)/shard_map/add | solution.py:296
  (5 shorter events, 0.1 us)
Async XLA Ops:
  14.6 4.0 %collective-permute-start = (bf16[4,4,32,768]{3,2,1,0:T(8,128)(2,1)S(1)}, bf16[4,4,32,768]{3,2,1,0:T(8,128)(2,1)S(1)}, u32[]{:S(2)}, u32[]{:S(2)}) collective-permute-start(bf16[4,4,32,768]{3,2,1,0:T(8,128)(2,1)S(1)} %get-tuple-element.25), channel_id=1, source_target_pairs={{0,1},{1,0},{2,3},{3,2},{4,5},{5,4},{6,7},{7,6},{8,9},{9,8},{10,11... | collective-permute-start | bytes 2359304 | tf_op jit(solution)/shard_map/ppermute | solution.py:18
  15.1 2.0 %copy-start.2 = (bf16[64,128]{1,0:T(8,128)(2,1)S(1)}, bf16[64,128]{1,0:T(8,128)(2,1)}, u32[]{:S(2)}) copy-start(bf16[64,128]{1,0:T(8,128)(2,1)} %scale_ref.4) | copy-start | bytes 49156
  15.1 2.0 %copy-start = (bf16[64,128,128]{2,1,0:T(8,128)(2,1)S(1)}, bf16[64,128,128]{2,1,0:T(8,128)(2,1)}, u32[]{:S(2)}) copy-start(bf16[64,128,128]{2,1,0:T(8,128)(2,1)} %self_ref.2) | copy-start | bytes 6291460
  17.0 1.6 %collective-permute-start.1 = (bf16[4,4,32,256]{3,2,1,0:T(8,128)(2,1)S(1)}, bf16[4,4,32,256]{3,2,1,0:T(8,128)(2,1)S(1)}, u32[]{:S(2)}, u32[]{:S(2)}) collective-permute-start(bf16[4,4,32,256]{3,2,1,0:T(8,128)(2,1)S(1)} %get-tuple-element.29), channel_id=1, source_target_pairs={{0,1},{1,0},{2,3},{3,2},{4,5},{5,4},{6,7},{7,6},{8,9},{9,8},{10,11... | collective-permute-start | bytes 786440 | tf_op jit(solution)/shard_map/ppermute | solution.py:18
  18.9 6.2 %copy-start.1 = (bf16[64,128,128]{2,1,0:T(8,128)(2,1)S(1)}, bf16[64,128,128]{2,1,0:T(8,128)(2,1)}, u32[]{:S(2)}) copy-start(bf16[64,128,128]{2,1,0:T(8,128)(2,1)} %prev_ref.2) | copy-start | bytes 6291460
  19.1 10.8 %collective-permute-start.2 = (bf16[4,32,1024]{2,1,0:T(8,128)(2,1)S(1)}, bf16[4,32,1024]{2,1,0:T(8,128)(2,1)S(1)}, u32[]{:S(2)}, u32[]{:S(2)}) collective-permute-start(bf16[4,32,1024]{2,1,0:T(8,128)(2,1)S(1)} %get-tuple-element.45), channel_id=1, source_target_pairs={{0,6},{2,4},{4,2},{6,0},{1,7},{3,5},{5,3},{7,1},{8,14},{10,12},{12... | collective-permute-start | bytes 786440 | tf_op jit(solution)/shard_map/ppermute | solution.py:18
  22.8 12.4 %collective-permute-start.3 = (bf16[4,32,1024]{2,1,0:T(8,128)(2,1)S(1)}, bf16[4,32,1024]{2,1,0:T(8,128)(2,1)S(1)}, u32[]{:S(2)}, u32[]{:S(2)}) collective-permute-start(bf16[4,32,1024]{2,1,0:T(8,128)(2,1)S(1)} %get-tuple-element.47), channel_id=1, source_target_pairs={{0,4},{2,6},{4,0},{6,2},{1,5},{3,7},{5,1},{7,3},{8,12},{10,14},{12... | collective-permute-start | bytes 786440 | tf_op jit(solution)/shard_map/ppermute | solution.py:18
  23.3 12.6 %collective-permute-start.4 = (bf16[4,32,1024]{2,1,0:T(8,128)(2,1)S(1)}, bf16[4,32,1024]{2,1,0:T(8,128)(2,1)S(1)}, u32[]{:S(2)}, u32[]{:S(2)}) collective-permute-start(bf16[4,32,1024]{2,1,0:T(8,128)(2,1)S(1)} %get-tuple-element.46), channel_id=1, source_target_pairs={{0,2},{2,0},{4,6},{6,4},{1,3},{3,1},{5,7},{7,5},{8,10},{10,8},{12,... | collective-permute-start | bytes 786440 | tf_op jit(solution)/shard_map/ppermute | solution.py:18
  23.4 12.6 %collective-permute-start.5 = (bf16[129,128]{1,0:T(8,128)(2,1)S(1)}, bf16[129,128]{1,0:T(8,128)(2,1)S(1)}, u32[]{:S(2)}, u32[]{:S(2)}) collective-permute-start(bf16[129,128]{1,0:T(8,128)(2,1)S(1)} %pad_maximum_fusion.1), channel_id=1, source_target_pairs={{0,1},{1,2},{2,3},{3,4},{4,5},{5,6},{6,7},{7,8},{8,9},{9,10},{10,1... | collective-permute-start | bytes 99080 | tf_op jit(solution)/shard_map/ppermute | solution.py:23
  36.0 4.3 %copy-start.3 = (bf16[129,128]{1,0:T(8,128)(2,1)}, bf16[129,128]{1,0:T(8,128)(2,1)S(1)}, u32[]{:S(2)}) copy-start(bf16[129,128]{1,0:T(8,128)(2,1)S(1)} %collective-permute-done.5.got_ref) | copy-start | bytes 99076
  36.1 7.7 %collective-permute-start.6 = (bf16[32,1024]{1,0:T(8,128)(2,1)S(1)}, bf16[32,1024]{1,0:T(8,128)(2,1)S(1)}, u32[]{:S(2)}, u32[]{:S(2)}) collective-permute-start(bf16[32,1024]{1,0:T(8,128)(2,1)S(1)} %get-tuple-element.48), channel_id=1, source_target_pairs={{0,16},{8,24},{16,0},{24,8},{1,17},{9,25},{17,1},{25,9},{2,18},{10... | collective-permute-start | bytes 196616 | tf_op jit(solution)/shard_map/ppermute | solution.py:18
  38.8 6.3 %collective-permute-start.7 = (bf16[32,1024]{1,0:T(8,128)(2,1)S(1)}, bf16[32,1024]{1,0:T(8,128)(2,1)S(1)}, u32[]{:S(2)}, u32[]{:S(2)}) collective-permute-start(bf16[32,1024]{1,0:T(8,128)(2,1)S(1)} %get-tuple-element.50), channel_id=1, source_target_pairs={{0,24},{8,16},{16,8},{24,0},{1,25},{9,17},{17,9},{25,1},{2,26},{10... | collective-permute-start | bytes 196616 | tf_op jit(solution)/shard_map/ppermute | solution.py:18
  40.1 5.2 %collective-permute-start.8 = (bf16[32,1024]{1,0:T(8,128)(2,1)S(1)}, bf16[32,1024]{1,0:T(8,128)(2,1)S(1)}, u32[]{:S(2)}, u32[]{:S(2)}) collective-permute-start(bf16[32,1024]{1,0:T(8,128)(2,1)S(1)} %get-tuple-element.49), channel_id=1, source_target_pairs={{0,8},{8,0},{16,24},{24,16},{1,9},{9,1},{17,25},{25,17},{2,10},{10... | collective-permute-start | bytes 196616 | tf_op jit(solution)/shard_map/ppermute | solution.py:18

commit v2 on v1

--- a/solution.py
+++ b/solution.py
@@ -57,7 +57,7 @@
         def one(v, carry, m=m):
             chip = (var ^ v) * n_own + (own ^ m)
             slot = (m, v) if order == "own" else (v, m)
-            keep_ref[slot] = acc[pl.ds(pl.multiple_of((2 * chip + sub) * held, held), held), :]
+            keep_ref[slot] = acc[pl.ds(pl.multiple_of((2 * chip + sub) * held, held), held), :].astype(keep_ref.dtype)
             send_ref[slot] = acc[pl.ds(pl.multiple_of((2 * chip + 1 - sub) * held, held), held), :].astype(send_ref.dtype)
             return carry
 
@@ -135,7 +135,7 @@
 
     def shapes(columns, order):
         lead = (n_own, n_var) if order == "own" else (n_var, n_own)
-        return [jax.ShapeDtypeStruct(lead + (held, columns), t) for t in (F32, sent)]
+        return [jax.ShapeDtypeStruct(lead + (held, columns), t) for t in (sent, sent)]
 
     hbm = pl.BlockSpec(memory_space=pltpu.HBM)
     smem, vmem = pl.BlockSpec(memory_space=pltpu.SMEM), pl.BlockSpec(memory_space=pltpu.VMEM)
@@ -172,6 +172,36 @@
     return [(keep, send.astype(BF16)) for keep, send in (first, second)]
 
 
+def join_kernel(n_parts, *refs):
+    kept, received, outs = refs[:n_parts], refs[n_parts : 2 * n_parts], refs[2 * n_parts :]
+
+    def one(v, carry):
+        for m in range(kept[0].shape[0]):
+            out, low = outs[m], 0
+            for keep_ref, got_ref in zip(kept, received):
+                high = low + keep_ref.shape[3]
+                out[v, :, low:high] = (keep_ref[m, v].astype(F32) + got_ref[m, v].astype(F32)).astype(out.dtype)
+                low = high
+        return carry
+
+    lax.fori_loop(0, kept[0].shape[1], one, 0)
+
+
+def join(kept, received):
+    n_own, n_var, held = kept[0].shape[:3]
+    side = sum(x.shape[3] for x in kept)
+    sent = BF16 if held % 16 == 0 else F32
+    vmem = pl.BlockSpec(memory_space=pltpu.VMEM)
+    return pl.pallas_call(
+        functools.partial(join_kernel, len(kept)),
+        out_shape=[jax.ShapeDtypeStruct((n_var, held, side), sent if m else F32) for m in range(n_own)],
+        in_specs=[vmem] * (2 * len(kept)),
+        out_specs=[vmem] * n_own,
+        compiler_params=pltpu.CompilerParams(vmem_limit_bytes=16 * 2**20),
+        name="join",
+    )(*kept, *received)
+
+
 def cover_kernel(group, self_ref, prev_ref, scale_ref, diag_out, lower_out, scale, diag, lower, sems):
     count, width = self_ref.shape[:2]
     scale[pl.ds(0, 8), :] = jnp.zeros((8, width), F32)
@@ -289,7 +319,7 @@
     sums = capacity(capacity_blocks, capacity_rows, scaling, side // 4 * 3, ("own", "own"))
     received = [swap(send, "sub", 1) for _, send in sums]
     received, tail, covered = lax.optimization_barrier((received, tail, (cover_self, cover_prev, scaling)))
-    total = jnp.concatenate([keep + term.astype(F32) for (keep, _), term in zip(sums, received)], axis=-1)
+    total = join([keep for keep, _ in sums], received)
     got = shifted(tail, AXES, 1)
     for axis in ("own", "var"):
         arrived = [swap(total[m].astype(BF16), axis, m) for m in send_order(axis)]

time: 46.2 us -> 46 us (level)
  no operation moved by 1% of the time
where the time goes in v2:
time: 46 us; the launch traced here: 45.7 us
  Pallas kernels  22.3 us (48%)
  starting transfers between devices  10.9 us (24%)
  waiting for transfers between devices  10.9 us (24%)
  other arithmetic  0.86 us (2%)
  between operations  0.76 us (2%)
    pallas_call x1, Pallas kernels, capacity(): pl.pallas_call(functools.partial(left_kernel, step, orders[0]), out_shape...  13.9 us
    ppermute x8, waiting for transfers between devices, swap(): return lax.ppermute(value, axis, [(i, i ^ mask) for i in range(count)])  10.9 us
    ppermute x8, starting transfers between devices, swap(): return lax.ppermute(value, axis, [(i, i ^ mask) for i in range(count)])  9.17 us
    pallas_call x1, Pallas kernels, cover(): pl.pallas_call(functools.partial(cover_kernel, group), out_shape=[jax.Sha...  3.86 us
    pallas_call x1, Pallas kernels, first_cover(): pl.pallas_call(first_kernel, out_shape=[jax.ShapeDtypeStruct(x.shape, x.d...  2.39 us
    pallas_call x1, Pallas kernels, capacity(): pl.pallas_call(functools.partial(right_kernel, step, orders[1]), out_shap...  1.89 us
    ppermute x1, starting transfers between devices, shifted(): lax.ppermute(value, axis, [(i, i + steps) for i in range(count - steps)])  1.69 us
  transfers between devices with their start and end apart: 9, of which 7 were waited for; matrix products, arithmetic and copies ran while one was open for 0% of the time, Pallas kernels for 18%

profile of v2, /device:TPU:0, one launch (start us, length us, event | category | flops | bytes accessed | tf_op | source)
XLA Modules:
  0.0 45.7 jit_solution(219233098000419338)
XLA Ops:
  0.6 13.9 %capacity_left.1 = (bf16[64,1024,128]{2,1,0:T(8,128)(2,1)S(1)}, f32[64,128]{1,0:T(8,128)S(1)}, f32[1024,768]{1,0:T(8,128)S(1)}, bf16[4,4,32,768]{3,2,1,0:T(8,128)(2,1)S(1)}, bf16[4,4,32,768]{3,2,1,0:T(8,128)(2,1)S(1)}) custom-call(s32[5,64]{1,0:T(8,128)} %bitcast.17, bf16[64,640,128]{2,1,0:T(8,128)(2,1)} %bitcast.16, bf16[64,128]{1,0:T(8,128)(2,1)} %scale_ref.4), custom_call_target="tpu_custom_call" | custom-call | flops 12884901888 | bytes 14680064 | tf_op jit(solution)/shard_map/capacity_left/pallas_call | solution.py:143
  14.6 0.5 %collective-permute-start = (bf16[4,4,32,768]{3,2,1,0:T(8,128)(2,1)S(1)}, bf16[4,4,32,768]{3,2,1,0:T(8,128)(2,1)S(1)}, u32[]{:S(2)}, u32[]{:S(2)}) collective-permute-start(bf16[4,4,32,768]{3,2,1,0:T(8,128)(2,1)S(1)} %get-tuple-element.33), channel_id=1, source_target_pairs={{0,1},{1,0},{2,3},{3,2},{4,5},{5,4},{6,7},{7,6},{8,9},{9,8},{10,11... | collective-permute-start | bytes 2359304 | tf_op jit(solution)/shard_map/ppermute | solution.py:18
  15.1 0.0 copy-start.2
  15.1 0.0 copy-start
  15.1 1.9 %capacity_right.1 = (bf16[4,4,32,256]{3,2,1,0:T(8,128)(2,1)S(1)}, bf16[4,4,32,256]{3,2,1,0:T(8,128)(2,1)S(1)}) custom-call(bf16[64,1024,128]{2,1,0:T(8,128)(2,1)S(1)} %get-tuple-element.29.dense, f32[64,128]{1,0:T(8,128)S(1)} %get-tuple-element.30.scale, f32[1024,768]{1,0:T(8,128)S(1)} %get-tuple-element.31.before), custom_call_target="tpu_custom_call" | custom-call | flops 12884901888 | bytes 1048576 | tf_op jit(solution)/shard_map/capacity_right/pallas_call | solution.py:162
  17.0 0.0 copy-start.1
  17.0 0.1 collective-permute-start.1
  17.1 0.0 copy-done.2
  17.1 0.0 copy-done
  17.1 1.4 %collective-permute-done.1.refs_3_ = bf16[4,4,32,256]{3,2,1,0:T(8,128)(2,1)S(1)} collective-permute-done((bf16[4,4,32,256]{3,2,1,0:T(8,128)(2,1)S(1)}, bf16[4,4,32,256]{3,2,1,0:T(8,128)(2,1)S(1)}, u32[]{:S(2)}, u32[]{:S(2)}) %collective-permute-start.1) | collective-permute-done | bytes 262176 | tf_op jit(solution)/shard_map/ppermute | solution.py:18
  18.6 0.0 collective-permute-done.refs_2_
  18.6 0.2 join.1
  18.8 3.7 %collective-permute-start.2 = (bf16[4,32,1024]{2,1,0:T(8,128)(2,1)S(1)}, bf16[4,32,1024]{2,1,0:T(8,128)(2,1)S(1)}, u32[]{:S(2)}, u32[]{:S(2)}) collective-permute-start(bf16[4,32,1024]{2,1,0:T(8,128)(2,1)S(1)} %get-tuple-element.38), channel_id=1, source_target_pairs={{0,6},{2,4},{4,2},{6,0},{1,7},{3,5},{5,3},{7,1},{8,14},{10,12},{12... | collective-permute-start | bytes 786440 | tf_op jit(solution)/shard_map/ppermute | solution.py:18
  22.5 0.5 %collective-permute-start.3 = (bf16[4,32,1024]{2,1,0:T(8,128)(2,1)S(1)}, bf16[4,32,1024]{2,1,0:T(8,128)(2,1)S(1)}, u32[]{:S(2)}, u32[]{:S(2)}) collective-permute-start(bf16[4,32,1024]{2,1,0:T(8,128)(2,1)S(1)} %get-tuple-element.39), channel_id=1, source_target_pairs={{0,4},{2,6},{4,0},{6,2},{1,5},{3,7},{5,1},{7,3},{8,12},{10,14},{12... | collective-permute-start | bytes 786440 | tf_op jit(solution)/shard_map/ppermute | solution.py:18
  23.0 0.1 collective-permute-start.4
  23.1 1.7 %collective-permute-start.5 = (bf16[129,128]{1,0:T(8,128)(2,1)S(1)}, bf16[129,128]{1,0:T(8,128)(2,1)S(1)}, u32[]{:S(2)}, u32[]{:S(2)}) collective-permute-start(bf16[129,128]{1,0:T(8,128)(2,1)S(1)} %pad_maximum_fusion), channel_id=1, source_target_pairs={{0,1},{1,2},{2,3},{3,4},{4,5},{5,6},{6,7},{7,8},{8,9},{9,10},{10,1... | collective-permute-start | bytes 99080 | tf_op jit(solution)/shard_map/ppermute | solution.py:23
  24.8 0.0 copy-done.1
  24.8 3.9 %cover.1 = (bf16[64,128,128]{2,1,0:T(8,128)(2,1)}, bf16[64,128,128]{2,1,0:T(8,128)(2,1)}) custom-call(bf16[64,128,128]{2,1,0:T(8,128)(2,1)S(1)} %copy-done, bf16[64,128,128]{2,1,0:T(8,128)(2,1)S(1)} %copy-done.1, bf16[64,128]{1,0:T(8,128)(2,1)S(1)} %copy-done.2), custom_call_target="tpu_custom_call" | custom-call | flops 1073741824 | bytes 8388608 | tf_op jit(solution)/shard_map/cover/pallas_call | solution.py:280
  28.7 1.0 %collective-permute-done.2 = bf16[4,32,1024]{2,1,0:T(8,128)(2,1)S(1)} collective-permute-done((bf16[4,32,1024]{2,1,0:T(8,128)(2,1)S(1)}, bf16[4,32,1024]{2,1,0:T(8,128)(2,1)S(1)}, u32[]{:S(2)}, u32[]{:S(2)}) %collective-permute-start.2) | collective-permute-done | bytes 262176 | tf_op jit(solution)/shard_map/ppermute | solution.py:18
  29.7 5.3 %collective-permute-done.3 = bf16[4,32,1024]{2,1,0:T(8,128)(2,1)S(1)} collective-permute-done((bf16[4,32,1024]{2,1,0:T(8,128)(2,1)S(1)}, bf16[4,32,1024]{2,1,0:T(8,128)(2,1)S(1)}, u32[]{:S(2)}, u32[]{:S(2)}) %collective-permute-start.3) | collective-permute-done | bytes 262176 | tf_op jit(solution)/shard_map/ppermute | solution.py:18
  34.9 0.7 %collective-permute-done.4 = bf16[4,32,1024]{2,1,0:T(8,128)(2,1)S(1)} collective-permute-done((bf16[4,32,1024]{2,1,0:T(8,128)(2,1)S(1)}, bf16[4,32,1024]{2,1,0:T(8,128)(2,1)S(1)}, u32[]{:S(2)}, u32[]{:S(2)}) %collective-permute-start.4) | collective-permute-done | bytes 262176 | tf_op jit(solution)/shard_map/ppermute | solution.py:18
  35.6 0.1 convert_add_fusion
  35.7 0.0 collective-permute-done.5.got_ref
  35.8 0.0 copy-start.3
  35.8 2.7 %collective-permute-start.6 = (bf16[32,1024]{1,0:T(8,128)(2,1)S(1)}, bf16[32,1024]{1,0:T(8,128)(2,1)S(1)}, u32[]{:S(2)}, u32[]{:S(2)}) collective-permute-start(bf16[32,1024]{1,0:T(8,128)(2,1)S(1)} %get-tuple-element.53), channel_id=1, source_target_pairs={{0,16},{8,24},{16,0},{24,8},{1,17},{9,25},{17,1},{25,9},{2,18},{10... | collective-permute-start | bytes 196616 | tf_op jit(solution)/shard_map/ppermute | solution.py:18
  38.5 1.3 %collective-permute-start.7 = (bf16[32,1024]{1,0:T(8,128)(2,1)S(1)}, bf16[32,1024]{1,0:T(8,128)(2,1)S(1)}, u32[]{:S(2)}, u32[]{:S(2)}) collective-permute-start(bf16[32,1024]{1,0:T(8,128)(2,1)S(1)} %get-tuple-element.55), channel_id=1, source_target_pairs={{0,24},{8,16},{16,8},{24,0},{1,25},{9,17},{17,9},{25,1},{2,26},{10... | collective-permute-start | bytes 196616 | tf_op jit(solution)/shard_map/ppermute | solution.py:18
  39.8 0.2 collective-permute-start.8
  40.1 0.0 copy-done.3
  40.1 2.4 %first_cover.1 = (bf16[64,128,128]{2,1,0:T(8,128)(2,1)}, bf16[64,128,128]{2,1,0:T(8,128)(2,1)}) custom-call(bf16[64,128,128]{2,1,0:T(8,128)(2,1)} %self_ref.2, bf16[64,128,128]{2,1,0:T(8,128)(2,1)} %prev_ref.2, bf16[64,128]{1,0:T(8,128)(2,1)} %scale_ref.4, bf16[129,128]{1,0:T(8,128)(2,1)} %copy-done.3, ...), custom_call_target="tpu_custom_call", output_to_operand_aliasing={{0}: (4, {}), {1}: (5, {})} | custom-call | tf_op jit(solution)/shard_map/first_cover/pallas_call | solution.py:304
  42.5 1.0 %collective-permute-done.6 = bf16[32,1024]{1,0:T(8,128)(2,1)S(1)} collective-permute-done((bf16[32,1024]{1,0:T(8,128)(2,1)S(1)}, bf16[32,1024]{1,0:T(8,128)(2,1)S(1)}, u32[]{:S(2)}, u32[]{:S(2)}) %collective-permute-start.6) | collective-permute-done | bytes 65568 | tf_op jit(solution)/shard_map/ppermute | solution.py:18
  43.5 1.3 %collective-permute-done.7 = bf16[32,1024]{1,0:T(8,128)(2,1)S(1)} collective-permute-done((bf16[32,1024]{1,0:T(8,128)(2,1)S(1)}, bf16[32,1024]{1,0:T(8,128)(2,1)S(1)}, u32[]{:S(2)}, u32[]{:S(2)}) %collective-permute-start.7) | collective-permute-done | bytes 65568 | tf_op jit(solution)/shard_map/ppermute | solution.py:18
  44.8 0.2 collective-permute-done.8
  45.0 0.7 %fusion.1 = f32[32,1024]{1,0:T(8,128)} fusion(bf16[32,1024]{1,0:T(8,128)(2,1)S(1)} %collective-permute-done.8, bf16[32,1024]{1,0:T(8,128)(2,1)S(1)} %collective-permute-done.7, bf16[32,1024]{1,0:T(8,128)(2,1)S(1)} %collective-permute-done.6, f32[4,32,1024]{2,1,0:T(8,128)S(1)} %convert_add_fusion), kind=kLoop, calls=%fused_computation.3 | loop fusion | flops 196608 | bytes 458752 | tf_op jit(solution)/shard_map/add | solution.py:326
  (5 shorter events, 0.1 us)
Async XLA Ops:
  14.6 4.0 %collective-permute-start = (bf16[4,4,32,768]{3,2,1,0:T(8,128)(2,1)S(1)}, bf16[4,4,32,768]{3,2,1,0:T(8,128)(2,1)S(1)}, u32[]{:S(2)}, u32[]{:S(2)}) collective-permute-start(bf16[4,4,32,768]{3,2,1,0:T(8,128)(2,1)S(1)} %get-tuple-element.33), channel_id=1, source_target_pairs={{0,1},{1,0},{2,3},{3,2},{4,5},{5,4},{6,7},{7,6},{8,9},{9,8},{10,11... | collective-permute-start | bytes 2359304 | tf_op jit(solution)/shard_map/ppermute | solution.py:18
  15.1 2.0 %copy-start.2 = (bf16[64,128]{1,0:T(8,128)(2,1)S(1)}, bf16[64,128]{1,0:T(8,128)(2,1)}, u32[]{:S(2)}) copy-start(bf16[64,128]{1,0:T(8,128)(2,1)} %scale_ref.4) | copy-start | bytes 49156
  15.1 2.0 %copy-start = (bf16[64,128,128]{2,1,0:T(8,128)(2,1)S(1)}, bf16[64,128,128]{2,1,0:T(8,128)(2,1)}, u32[]{:S(2)}) copy-start(bf16[64,128,128]{2,1,0:T(8,128)(2,1)} %self_ref.2) | copy-start | bytes 6291460
  17.0 7.9 %copy-start.1 = (bf16[64,128,128]{2,1,0:T(8,128)(2,1)S(1)}, bf16[64,128,128]{2,1,0:T(8,128)(2,1)}, u32[]{:S(2)}) copy-start(bf16[64,128,128]{2,1,0:T(8,128)(2,1)} %prev_ref.2) | copy-start | bytes 6291460
  17.0 1.6 %collective-permute-start.1 = (bf16[4,4,32,256]{3,2,1,0:T(8,128)(2,1)S(1)}, bf16[4,4,32,256]{3,2,1,0:T(8,128)(2,1)S(1)}, u32[]{:S(2)}, u32[]{:S(2)}) collective-permute-start(bf16[4,4,32,256]{3,2,1,0:T(8,128)(2,1)S(1)} %get-tuple-element.34), channel_id=1, source_target_pairs={{0,1},{1,0},{2,3},{3,2},{4,5},{5,4},{6,7},{7,6},{8,9},{9,8},{10,11... | collective-permute-start | bytes 786440 | tf_op jit(solution)/shard_map/ppermute | solution.py:18
  18.8 10.8 %collective-permute-start.2 = (bf16[4,32,1024]{2,1,0:T(8,128)(2,1)S(1)}, bf16[4,32,1024]{2,1,0:T(8,128)(2,1)S(1)}, u32[]{:S(2)}, u32[]{:S(2)}) collective-permute-start(bf16[4,32,1024]{2,1,0:T(8,128)(2,1)S(1)} %get-tuple-element.38), channel_id=1, source_target_pairs={{0,6},{2,4},{4,2},{6,0},{1,7},{3,5},{5,3},{7,1},{8,14},{10,12},{12... | collective-permute-start | bytes 786440 | tf_op jit(solution)/shard_map/ppermute | solution.py:18
  22.5 12.4 %collective-permute-start.3 = (bf16[4,32,1024]{2,1,0:T(8,128)(2,1)S(1)}, bf16[4,32,1024]{2,1,0:T(8,128)(2,1)S(1)}, u32[]{:S(2)}, u32[]{:S(2)}) collective-permute-start(bf16[4,32,1024]{2,1,0:T(8,128)(2,1)S(1)} %get-tuple-element.39), channel_id=1, source_target_pairs={{0,4},{2,6},{4,0},{6,2},{1,5},{3,7},{5,1},{7,3},{8,12},{10,14},{12... | collective-permute-start | bytes 786440 | tf_op jit(solution)/shard_map/ppermute | solution.py:18
  23.0 12.6 %collective-permute-start.4 = (bf16[4,32,1024]{2,1,0:T(8,128)(2,1)S(1)}, bf16[4,32,1024]{2,1,0:T(8,128)(2,1)S(1)}, u32[]{:S(2)}, u32[]{:S(2)}) collective-permute-start(bf16[4,32,1024]{2,1,0:T(8,128)(2,1)S(1)} %get-tuple-element.40), channel_id=1, source_target_pairs={{0,2},{2,0},{4,6},{6,4},{1,3},{3,1},{5,7},{7,5},{8,10},{10,8},{12,... | collective-permute-start | bytes 786440 | tf_op jit(solution)/shard_map/ppermute | solution.py:18
  23.1 12.6 %collective-permute-start.5 = (bf16[129,128]{1,0:T(8,128)(2,1)S(1)}, bf16[129,128]{1,0:T(8,128)(2,1)S(1)}, u32[]{:S(2)}, u32[]{:S(2)}) collective-permute-start(bf16[129,128]{1,0:T(8,128)(2,1)S(1)} %pad_maximum_fusion), channel_id=1, source_target_pairs={{0,1},{1,2},{2,3},{3,4},{4,5},{5,6},{6,7},{7,8},{8,9},{9,10},{10,1... | collective-permute-start | bytes 99080 | tf_op jit(solution)/shard_map/ppermute | solution.py:23
  35.8 4.3 %copy-start.3 = (bf16[129,128]{1,0:T(8,128)(2,1)}, bf16[129,128]{1,0:T(8,128)(2,1)S(1)}, u32[]{:S(2)}) copy-start(bf16[129,128]{1,0:T(8,128)(2,1)S(1)} %collective-permute-done.5.got_ref) | copy-start | bytes 99076
  35.8 7.7 %collective-permute-start.6 = (bf16[32,1024]{1,0:T(8,128)(2,1)S(1)}, bf16[32,1024]{1,0:T(8,128)(2,1)S(1)}, u32[]{:S(2)}, u32[]{:S(2)}) collective-permute-start(bf16[32,1024]{1,0:T(8,128)(2,1)S(1)} %get-tuple-element.53), channel_id=1, source_target_pairs={{0,16},{8,24},{16,0},{24,8},{1,17},{9,25},{17,1},{25,9},{2,18},{10... | collective-permute-start | bytes 196616 | tf_op jit(solution)/shard_map/ppermute | solution.py:18
  38.5 6.3 %collective-permute-start.7 = (bf16[32,1024]{1,0:T(8,128)(2,1)S(1)}, bf16[32,1024]{1,0:T(8,128)(2,1)S(1)}, u32[]{:S(2)}, u32[]{:S(2)}) collective-permute-start(bf16[32,1024]{1,0:T(8,128)(2,1)S(1)} %get-tuple-element.55), channel_id=1, source_target_pairs={{0,24},{8,16},{16,8},{24,0},{1,25},{9,17},{17,9},{25,1},{2,26},{10... | collective-permute-start | bytes 196616 | tf_op jit(solution)/shard_map/ppermute | solution.py:18
  39.8 5.2 %collective-permute-start.8 = (bf16[32,1024]{1,0:T(8,128)(2,1)S(1)}, bf16[32,1024]{1,0:T(8,128)(2,1)S(1)}, u32[]{:S(2)}, u32[]{:S(2)}) collective-permute-start(bf16[32,1024]{1,0:T(8,128)(2,1)S(1)} %get-tuple-element.54), channel_id=1, source_target_pairs={{0,8},{8,0},{16,24},{24,16},{1,9},{9,1},{17,25},{25,17},{2,10},{10... | collective-permute-start | bytes 196616 | tf_op jit(solution)/shard_map/ppermute | solution.py:18

commit v3 on v2

--- a/solution.py
+++ b/solution.py
@@ -112,12 +112,7 @@
     count, tile = dense.shape[0], 2 * dense.shape[2]
     low = before.shape[1] // tile
     acc[...] = jnp.zeros_like(acc)
-
-    def turn(t, carry):
-        multiply(dense, scale, acc, [t * step + i for i in range(step)], low, tile)
-        return carry
-
-    lax.fori_loop(0, count // step, turn, 0)
+    multiply(dense, scale, acc, range(count), low, tile)
     for j in range(low, low + acc.shape[1] // tile):
         for i in range(j):
             source, at = (before, i) if i < low else (acc, i - low)

time: 46 us -> 45.5 us (0.989)
  Pallas kernels: 22.3 us -> 21.8 us
    pallas_call x1, Pallas kernels: 1.89 us -> 1.34 us  [capacity(): pl.pallas_call(functools.partial(right_kernel, step, orders[1]), out_shap...]
  transfers between devices with their start and end apart: 9 -> 9, of which waited for: 7 -> 7; matrix products, arithmetic and copies ran while one was open for 0% -> 0% of each run, Pallas kernels for 18% -> 17%
where the time goes in v3:
time: 45.5 us; the launch traced here: 45.1 us
  Pallas kernels  21.8 us (48%)
  starting transfers between devices  10.9 us (24%)
  waiting for transfers between devices  10.8 us (24%)
  other arithmetic  0.86 us (2%)
  between operations  0.74 us (2%)
    pallas_call x1, Pallas kernels, capacity(): pl.pallas_call(functools.partial(left_kernel, step, orders[0]), out_shape...  13.9 us
    ppermute x8, waiting for transfers between devices, swap(): return lax.ppermute(value, axis, [(i, i ^ mask) for i in range(count)])  10.8 us
    ppermute x8, starting transfers between devices, swap(): return lax.ppermute(value, axis, [(i, i ^ mask) for i in range(count)])  9.17 us
    pallas_call x1, Pallas kernels, cover(): pl.pallas_call(functools.partial(cover_kernel, group), out_shape=[jax.Sha...  3.86 us
    pallas_call x1, Pallas kernels, first_cover(): pl.pallas_call(first_kernel, out_shape=[jax.ShapeDtypeStruct(x.shape, x.d...  2.39 us
    ppermute x1, starting transfers between devices, shifted(): lax.ppermute(value, axis, [(i, i + steps) for i in range(count - steps)])  1.69 us
    pallas_call x1, Pallas kernels, capacity(): pl.pallas_call(functools.partial(right_kernel, step, orders[1]), out_shap...  1.34 us
  transfers between devices with their start and end apart: 9, of which 7 were waited for; matrix products, arithmetic and copies ran while one was open for 0% of the time, Pallas kernels for 17%

profile of v3, /device:TPU:0, one launch (start us, length us, event | category | flops | bytes accessed | tf_op | source)
XLA Modules:
  0.0 45.1 jit_solution(17657099432219028368)
XLA Ops:
  0.6 13.9 %capacity_left.1 = (bf16[64,1024,128]{2,1,0:T(8,128)(2,1)S(1)}, f32[64,128]{1,0:T(8,128)S(1)}, f32[1024,768]{1,0:T(8,128)S(1)}, bf16[4,4,32,768]{3,2,1,0:T(8,128)(2,1)S(1)}, bf16[4,4,32,768]{3,2,1,0:T(8,128)(2,1)S(1)}) custom-call(s32[5,64]{1,0:T(8,128)} %bitcast.17, bf16[64,640,128]{2,1,0:T(8,128)(2,1)} %bitcast.16, bf16[64,128]{1,0:T(8,128)(2,1)} %scale_ref.4), custom_call_target="tpu_custom_call" | custom-call | flops 12884901888 | bytes 14680064 | tf_op jit(solution)/shard_map/capacity_left/pallas_call | solution.py:138
  14.6 0.5 %collective-permute-start = (bf16[4,4,32,768]{3,2,1,0:T(8,128)(2,1)S(1)}, bf16[4,4,32,768]{3,2,1,0:T(8,128)(2,1)S(1)}, u32[]{:S(2)}, u32[]{:S(2)}) collective-permute-start(bf16[4,4,32,768]{3,2,1,0:T(8,128)(2,1)S(1)} %get-tuple-element.33), channel_id=1, source_target_pairs={{0,1},{1,0},{2,3},{3,2},{4,5},{5,4},{6,7},{7,6},{8,9},{9,8},{10,11... | collective-permute-start | bytes 2359304 | tf_op jit(solution)/shard_map/ppermute | solution.py:18
  15.1 0.0 copy-start.2
  15.1 0.0 copy-start
  15.1 1.3 %capacity_right.1 = (bf16[4,4,32,256]{3,2,1,0:T(8,128)(2,1)S(1)}, bf16[4,4,32,256]{3,2,1,0:T(8,128)(2,1)S(1)}) custom-call(bf16[64,1024,128]{2,1,0:T(8,128)(2,1)S(1)} %get-tuple-element.29.dense, f32[64,128]{1,0:T(8,128)S(1)} %get-tuple-element.30.scale, f32[1024,768]{1,0:T(8,128)S(1)} %get-tuple-element.31.before), custom_call_target="tpu_custom_call" | custom-call | flops 12884901888 | bytes 1048576 | tf_op jit(solution)/shard_map/capacity_right/pallas_call | solution.py:157
  16.4 0.0 copy-start.1
  16.4 0.1 collective-permute-start.1
  16.6 0.0 copy-done.2
  16.6 0.1 copy-done
  16.7 1.3 %collective-permute-done.1.refs_3_ = bf16[4,4,32,256]{3,2,1,0:T(8,128)(2,1)S(1)} collective-permute-done((bf16[4,4,32,256]{3,2,1,0:T(8,128)(2,1)S(1)}, bf16[4,4,32,256]{3,2,1,0:T(8,128)(2,1)S(1)}, u32[]{:S(2)}, u32[]{:S(2)}) %collective-permute-start.1) | collective-permute-done | bytes 262176 | tf_op jit(solution)/shard_map/ppermute | solution.py:18
  18.0 0.0 collective-permute-done.refs_2_
  18.0 0.2 join.1
  18.3 3.7 %collective-permute-start.2 = (bf16[4,32,1024]{2,1,0:T(8,128)(2,1)S(1)}, bf16[4,32,1024]{2,1,0:T(8,128)(2,1)S(1)}, u32[]{:S(2)}, u32[]{:S(2)}) collective-permute-start(bf16[4,32,1024]{2,1,0:T(8,128)(2,1)S(1)} %get-tuple-element.38), channel_id=1, source_target_pairs={{0,6},{2,4},{4,2},{6,0},{1,7},{3,5},{5,3},{7,1},{8,14},{10,12},{12... | collective-permute-start | bytes 786440 | tf_op jit(solution)/shard_map/ppermute | solution.py:18
  22.0 0.5 %collective-permute-start.3 = (bf16[4,32,1024]{2,1,0:T(8,128)(2,1)S(1)}, bf16[4,32,1024]{2,1,0:T(8,128)(2,1)S(1)}, u32[]{:S(2)}, u32[]{:S(2)}) collective-permute-start(bf16[4,32,1024]{2,1,0:T(8,128)(2,1)S(1)} %get-tuple-element.39), channel_id=1, source_target_pairs={{0,4},{2,6},{4,0},{6,2},{1,5},{3,7},{5,1},{7,3},{8,12},{10,14},{12... | collective-permute-start | bytes 786440 | tf_op jit(solution)/shard_map/ppermute | solution.py:18
  22.5 0.1 collective-permute-start.4
  22.6 1.7 %collective-permute-start.5 = (bf16[129,128]{1,0:T(8,128)(2,1)S(1)}, bf16[129,128]{1,0:T(8,128)(2,1)S(1)}, u32[]{:S(2)}, u32[]{:S(2)}) collective-permute-start(bf16[129,128]{1,0:T(8,128)(2,1)S(1)} %pad_maximum_fusion), channel_id=1, source_target_pairs={{0,1},{1,2},{2,3},{3,4},{4,5},{5,6},{6,7},{7,8},{8,9},{9,10},{10,1... | collective-permute-start | bytes 99080 | tf_op jit(solution)/shard_map/ppermute | solution.py:23
  24.3 0.0 copy-done.1
  24.3 3.9 %cover.1 = (bf16[64,128,128]{2,1,0:T(8,128)(2,1)}, bf16[64,128,128]{2,1,0:T(8,128)(2,1)}) custom-call(bf16[64,128,128]{2,1,0:T(8,128)(2,1)S(1)} %copy-done, bf16[64,128,128]{2,1,0:T(8,128)(2,1)S(1)} %copy-done.1, bf16[64,128]{1,0:T(8,128)(2,1)S(1)} %copy-done.2), custom_call_target="tpu_custom_call" | custom-call | flops 1073741824 | bytes 8388608 | tf_op jit(solution)/shard_map/cover/pallas_call | solution.py:275
  28.2 1.0 %collective-permute-done.2 = bf16[4,32,1024]{2,1,0:T(8,128)(2,1)S(1)} collective-permute-done((bf16[4,32,1024]{2,1,0:T(8,128)(2,1)S(1)}, bf16[4,32,1024]{2,1,0:T(8,128)(2,1)S(1)}, u32[]{:S(2)}, u32[]{:S(2)}) %collective-permute-start.2) | collective-permute-done | bytes 262176 | tf_op jit(solution)/shard_map/ppermute | solution.py:18
  29.1 5.3 %collective-permute-done.3 = bf16[4,32,1024]{2,1,0:T(8,128)(2,1)S(1)} collective-permute-done((bf16[4,32,1024]{2,1,0:T(8,128)(2,1)S(1)}, bf16[4,32,1024]{2,1,0:T(8,128)(2,1)S(1)}, u32[]{:S(2)}, u32[]{:S(2)}) %collective-permute-start.3) | collective-permute-done | bytes 262176 | tf_op jit(solution)/shard_map/ppermute | solution.py:18
  34.4 0.7 %collective-permute-done.4 = bf16[4,32,1024]{2,1,0:T(8,128)(2,1)S(1)} collective-permute-done((bf16[4,32,1024]{2,1,0:T(8,128)(2,1)S(1)}, bf16[4,32,1024]{2,1,0:T(8,128)(2,1)S(1)}, u32[]{:S(2)}, u32[]{:S(2)}) %collective-permute-start.4) | collective-permute-done | bytes 262176 | tf_op jit(solution)/shard_map/ppermute | solution.py:18
  35.1 0.1 convert_add_fusion
  35.2 0.0 collective-permute-done.5.got_ref
  35.2 0.0 copy-start.3
  35.3 2.7 %collective-permute-start.6 = (bf16[32,1024]{1,0:T(8,128)(2,1)S(1)}, bf16[32,1024]{1,0:T(8,128)(2,1)S(1)}, u32[]{:S(2)}, u32[]{:S(2)}) collective-permute-start(bf16[32,1024]{1,0:T(8,128)(2,1)S(1)} %get-tuple-element.53), channel_id=1, source_target_pairs={{0,16},{8,24},{16,0},{24,8},{1,17},{9,25},{17,1},{25,9},{2,18},{10... | collective-permute-start | bytes 196616 | tf_op jit(solution)/shard_map/ppermute | solution.py:18
  37.9 1.3 %collective-permute-start.7 = (bf16[32,1024]{1,0:T(8,128)(2,1)S(1)}, bf16[32,1024]{1,0:T(8,128)(2,1)S(1)}, u32[]{:S(2)}, u32[]{:S(2)}) collective-permute-start(bf16[32,1024]{1,0:T(8,128)(2,1)S(1)} %get-tuple-element.55), channel_id=1, source_target_pairs={{0,24},{8,16},{16,8},{24,0},{1,25},{9,17},{17,9},{25,1},{2,26},{10... | collective-permute-start | bytes 196616 | tf_op jit(solution)/shard_map/ppermute | solution.py:18
  39.3 0.2 collective-permute-start.8
  39.5 0.0 copy-done.3
  39.5 2.4 %first_cover.1 = (bf16[64,128,128]{2,1,0:T(8,128)(2,1)}, bf16[64,128,128]{2,1,0:T(8,128)(2,1)}) custom-call(bf16[64,128,128]{2,1,0:T(8,128)(2,1)} %self_ref.2, bf16[64,128,128]{2,1,0:T(8,128)(2,1)} %prev_ref.2, bf16[64,128]{1,0:T(8,128)(2,1)} %scale_ref.4, bf16[129,128]{1,0:T(8,128)(2,1)} %copy-done.3, ...), custom_call_target="tpu_custom_call", output_to_operand_aliasing={{0}: (4, {}), {1}: (5, {})} | custom-call | tf_op jit(solution)/shard_map/first_cover/pallas_call | solution.py:299
  41.9 1.0 %collective-permute-done.6 = bf16[32,1024]{1,0:T(8,128)(2,1)S(1)} collective-permute-done((bf16[32,1024]{1,0:T(8,128)(2,1)S(1)}, bf16[32,1024]{1,0:T(8,128)(2,1)S(1)}, u32[]{:S(2)}, u32[]{:S(2)}) %collective-permute-start.6) | collective-permute-done | bytes 65568 | tf_op jit(solution)/shard_map/ppermute | solution.py:18
  43.0 1.3 %collective-permute-done.7 = bf16[32,1024]{1,0:T(8,128)(2,1)S(1)} collective-permute-done((bf16[32,1024]{1,0:T(8,128)(2,1)S(1)}, bf16[32,1024]{1,0:T(8,128)(2,1)S(1)}, u32[]{:S(2)}, u32[]{:S(2)}) %collective-permute-start.7) | collective-permute-done | bytes 65568 | tf_op jit(solution)/shard_map/ppermute | solution.py:18
  44.3 0.2 collective-permute-done.8
  44.5 0.7 %fusion.1 = f32[32,1024]{1,0:T(8,128)} fusion(bf16[32,1024]{1,0:T(8,128)(2,1)S(1)} %collective-permute-done.8, bf16[32,1024]{1,0:T(8,128)(2,1)S(1)} %collective-permute-done.7, bf16[32,1024]{1,0:T(8,128)(2,1)S(1)} %collective-permute-done.6, f32[4,32,1024]{2,1,0:T(8,128)S(1)} %convert_add_fusion), kind=kLoop, calls=%fused_computation.3 | loop fusion | flops 196608 | bytes 458752 | tf_op jit(solution)/shard_map/add | solution.py:321
  (5 shorter events, 0.1 us)
Async XLA Ops:
  14.6 3.5 %collective-permute-start = (bf16[4,4,32,768]{3,2,1,0:T(8,128)(2,1)S(1)}, bf16[4,4,32,768]{3,2,1,0:T(8,128)(2,1)S(1)}, u32[]{:S(2)}, u32[]{:S(2)}) collective-permute-start(bf16[4,4,32,768]{3,2,1,0:T(8,128)(2,1)S(1)} %get-tuple-element.33), channel_id=1, source_target_pairs={{0,1},{1,0},{2,3},{3,2},{4,5},{5,4},{6,7},{7,6},{8,9},{9,8},{10,11... | collective-permute-start | bytes 2359304 | tf_op jit(solution)/shard_map/ppermute | solution.py:18
  15.1 1.5 %copy-start.2 = (bf16[64,128]{1,0:T(8,128)(2,1)S(1)}, bf16[64,128]{1,0:T(8,128)(2,1)}, u32[]{:S(2)}) copy-start(bf16[64,128]{1,0:T(8,128)(2,1)} %scale_ref.4) | copy-start | bytes 49156
  15.1 1.6 %copy-start = (bf16[64,128,128]{2,1,0:T(8,128)(2,1)S(1)}, bf16[64,128,128]{2,1,0:T(8,128)(2,1)}, u32[]{:S(2)}) copy-start(bf16[64,128,128]{2,1,0:T(8,128)(2,1)} %self_ref.2) | copy-start | bytes 6291460
  16.4 7.9 %copy-start.1 = (bf16[64,128,128]{2,1,0:T(8,128)(2,1)S(1)}, bf16[64,128,128]{2,1,0:T(8,128)(2,1)}, u32[]{:S(2)}) copy-start(bf16[64,128,128]{2,1,0:T(8,128)(2,1)} %prev_ref.2) | copy-start | bytes 6291460
  16.4 1.6 %collective-permute-start.1 = (bf16[4,4,32,256]{3,2,1,0:T(8,128)(2,1)S(1)}, bf16[4,4,32,256]{3,2,1,0:T(8,128)(2,1)S(1)}, u32[]{:S(2)}, u32[]{:S(2)}) collective-permute-start(bf16[4,4,32,256]{3,2,1,0:T(8,128)(2,1)S(1)} %get-tuple-element.34), channel_id=1, source_target_pairs={{0,1},{1,0},{2,3},{3,2},{4,5},{5,4},{6,7},{7,6},{8,9},{9,8},{10,11... | collective-permute-start | bytes 786440 | tf_op jit(solution)/shard_map/ppermute | solution.py:18
  18.3 10.8 %collective-permute-start.2 = (bf16[4,32,1024]{2,1,0:T(8,128)(2,1)S(1)}, bf16[4,32,1024]{2,1,0:T(8,128)(2,1)S(1)}, u32[]{:S(2)}, u32[]{:S(2)}) collective-permute-start(bf16[4,32,1024]{2,1,0:T(8,128)(2,1)S(1)} %get-tuple-element.38), channel_id=1, source_target_pairs={{0,6},{2,4},{4,2},{6,0},{1,7},{3,5},{5,3},{7,1},{8,14},{10,12},{12... | collective-permute-start | bytes 786440 | tf_op jit(solution)/shard_map/ppermute | solution.py:18
  22.0 12.4 %collective-permute-start.3 = (bf16[4,32,1024]{2,1,0:T(8,128)(2,1)S(1)}, bf16[4,32,1024]{2,1,0:T(8,128)(2,1)S(1)}, u32[]{:S(2)}, u32[]{:S(2)}) collective-permute-start(bf16[4,32,1024]{2,1,0:T(8,128)(2,1)S(1)} %get-tuple-element.39), channel_id=1, source_target_pairs={{0,4},{2,6},{4,0},{6,2},{1,5},{3,7},{5,1},{7,3},{8,12},{10,14},{12... | collective-permute-start | bytes 786440 | tf_op jit(solution)/shard_map/ppermute | solution.py:18
  22.5 12.6 %collective-permute-start.4 = (bf16[4,32,1024]{2,1,0:T(8,128)(2,1)S(1)}, bf16[4,32,1024]{2,1,0:T(8,128)(2,1)S(1)}, u32[]{:S(2)}, u32[]{:S(2)}) collective-permute-start(bf16[4,32,1024]{2,1,0:T(8,128)(2,1)S(1)} %get-tuple-element.40), channel_id=1, source_target_pairs={{0,2},{2,0},{4,6},{6,4},{1,3},{3,1},{5,7},{7,5},{8,10},{10,8},{12,... | collective-permute-start | bytes 786440 | tf_op jit(solution)/shard_map/ppermute | solution.py:18
  22.6 12.6 %collective-permute-start.5 = (bf16[129,128]{1,0:T(8,128)(2,1)S(1)}, bf16[129,128]{1,0:T(8,128)(2,1)S(1)}, u32[]{:S(2)}, u32[]{:S(2)}) collective-permute-start(bf16[129,128]{1,0:T(8,128)(2,1)S(1)} %pad_maximum_fusion), channel_id=1, source_target_pairs={{0,1},{1,2},{2,3},{3,4},{4,5},{5,6},{6,7},{7,8},{8,9},{9,10},{10,1... | collective-permute-start | bytes 99080 | tf_op jit(solution)/shard_map/ppermute | solution.py:23
  35.2 4.3 %copy-start.3 = (bf16[129,128]{1,0:T(8,128)(2,1)}, bf16[129,128]{1,0:T(8,128)(2,1)S(1)}, u32[]{:S(2)}) copy-start(bf16[129,128]{1,0:T(8,128)(2,1)S(1)} %collective-permute-done.5.got_ref) | copy-start | bytes 99076
  35.3 7.7 %collective-permute-start.6 = (bf16[32,1024]{1,0:T(8,128)(2,1)S(1)}, bf16[32,1024]{1,0:T(8,128)(2,1)S(1)}, u32[]{:S(2)}, u32[]{:S(2)}) collective-permute-start(bf16[32,1024]{1,0:T(8,128)(2,1)S(1)} %get-tuple-element.53), channel_id=1, source_target_pairs={{0,16},{8,24},{16,0},{24,8},{1,17},{9,25},{17,1},{25,9},{2,18},{10... | collective-permute-start | bytes 196616 | tf_op jit(solution)/shard_map/ppermute | solution.py:18
  37.9 6.3 %collective-permute-start.7 = (bf16[32,1024]{1,0:T(8,128)(2,1)S(1)}, bf16[32,1024]{1,0:T(8,128)(2,1)S(1)}, u32[]{:S(2)}, u32[]{:S(2)}) collective-permute-start(bf16[32,1024]{1,0:T(8,128)(2,1)S(1)} %get-tuple-element.55), channel_id=1, source_target_pairs={{0,24},{8,16},{16,8},{24,0},{1,25},{9,17},{17,9},{25,1},{2,26},{10... | collective-permute-start | bytes 196616 | tf_op jit(solution)/shard_map/ppermute | solution.py:18
  39.3 5.2 %collective-permute-start.8 = (bf16[32,1024]{1,0:T(8,128)(2,1)S(1)}, bf16[32,1024]{1,0:T(8,128)(2,1)S(1)}, u32[]{:S(2)}, u32[]{:S(2)}) collective-permute-start(bf16[32,1024]{1,0:T(8,128)(2,1)S(1)} %get-tuple-element.54), channel_id=1, source_target_pairs={{0,8},{8,0},{16,24},{24,16},{1,9},{9,1},{17,25},{25,17},{2,10},{10... | collective-permute-start | bytes 196616 | tf_op jit(solution)/shard_map/ppermute | solution.py:18
